TPU v7x, 32 devices: a whole 2x2x4 slice. The times are simulated.
32 devices in a mesh: img: 2 (over x), py: 4 (over y, core), px: 4 (over z).
Axes of the slice: x: 2, y: 2, z: 4, core: 2. Of those that a mesh axis runs over, the one named last changes fastest.
Arguments:
- queries: bfloat16 [2, 64, 64, 1536], P('img', 'py', 'px')
- keys: bfloat16 [2, 64, 64, 1536], P('img', 'py', 'px')
- values: bfloat16 [2, 64, 64, 1536], P('img', 'py', 'px'), may hold values from -6 to 6
- pattern: int32 [2, 8, 8, 9], P('img', 'py', 'px'), may hold values from 0 to 1, as said below
- targets: int32 [2, 8, 8, 12, 3], P('img', 'py', 'px'), may hold values from 0 to 8, as said below
- router_q: float32 [12, 128, 64], replicated, may hold values from -1.5 to 1.5
- router_k: float32 [12, 128, 64], replicated, may hold values from -1.5 to 1.5
Outputs:
- attended: bfloat16 [2, 64, 64, 1536], P('img', 'py', 'px')
- grad_q: float32 [12, 128, 64], replicated
- grad_k: float32 [12, 128, 64], replicated
Inputs may be any that keep to these rules, and one draw needn't show every extreme that they name: `pattern`: the centre offset and the offsets one block away along one axis that lie in the image are 1; offsets outside the image are 0. `targets`: 3 different offsets per query block and head, each with pattern 1.
All inputs are finite; a program needn't handle non-finite values.
Results may differ from a plain program's by a relative error of at most 0.0049.
Values may be sent and summed in bfloat16 or wider, within the bound.
A program may use at most 64 MiB of HBM per device.

v0:
```python
import math

import jax
import jax.numpy as jnp
from jax import lax
from jax.sharding import PartitionSpec as P

HEADS = 12
DH = 128
RW = 64
BS = 8
RADIUS = 1
TOPK = 3
NOFF = 9


def extended_2(cells, sides, width):
    for axis, dim in sides:
        count = lax.axis_size(axis)
        ends = count - 1
        head = lax.slice_in_dim(cells, 0, width, axis=dim)
        tail = lax.slice_in_dim(cells, cells.shape[dim] - width, cells.shape[dim], axis=dim)
        cells = jnp.concatenate(
            [
                lax.ppermute(tail, axis, [(i, (i + 1) % count) for i in range(ends)]),
                cells,
                lax.ppermute(head, axis, [((i + 1) % count, i) for i in range(ends)]),
            ],
            axis=dim,
        )
    return cells


def attend(query_tile, key_ext, value_ext, live):
    tile_y, tile_x, feat = query_tile.shape
    blocks_y = tile_y // BS
    blocks_x = tile_x // BS
    width = 2 * RADIUS + 1
    side = width * BS
    scale = 1.0 / math.sqrt(DH)
    anchor = jnp.zeros((), jnp.int32)

    def regroup(window):
        return (
            window.reshape(width, BS, width, BS, feat)
            .transpose(0, 2, 1, 3, 4)
            .reshape(NOFF * BS * BS, HEADS, DH)
        )

    def one_block(index):
        row = index // blocks_x
        col = index % blocks_x
        start_y = row * BS
        start_x = col * BS
        query = lax.dynamic_slice(query_tile, (start_y, start_x, anchor), (BS, BS, feat)).reshape(
            BS * BS, HEADS, DH
        )
        window_k = regroup(
            lax.dynamic_slice(key_ext, (start_y, start_x, anchor), (side, side, feat))
        )
        window_v = regroup(
            lax.dynamic_slice(value_ext, (start_y, start_x, anchor), (side, side, feat))
        )
        mask_row = lax.dynamic_slice(live, (row, col, anchor), (1, 1, NOFF)).reshape(NOFF)
        key_mask = jnp.repeat(mask_row, BS * BS) > 0
        scores = (
            jnp.einsum("qhd,khd->hqk", query, window_k, preferred_element_type=jnp.float32) * scale
        )
        scores = jnp.where(key_mask[None, None, :], scores, -1e30)
        top = jnp.max(scores, axis=-1, keepdims=True)
        weights = jnp.exp(scores - top)
        probs = (weights / jnp.sum(weights, axis=-1, keepdims=True)).astype(jnp.bfloat16)
        out = jnp.einsum("hqk,khd->qhd", probs, window_v, preferred_element_type=jnp.float32)
        return out.astype(jnp.bfloat16).reshape(BS, BS, feat)

    outs = lax.map(one_block, jnp.arange(blocks_y * blocks_x, dtype=jnp.int32))
    return (
        outs.reshape(blocks_y, blocks_x, BS, BS, feat)
        .transpose(0, 2, 1, 3, 4)
        .reshape(tile_y, tile_x, feat)
    )


def pooling(tile):
    tile_y, tile_x, feat = tile.shape
    shaped = tile.reshape(tile_y // BS, BS, tile_x // BS, BS, HEADS, DH)
    return jnp.sum(shaped, axis=(1, 3), dtype=jnp.float32) / (BS * BS)


def router_loss(weights_q, weights_k, pooled_q, pooled_k, live, chosen):
    route_q = jnp.einsum("yxhd,hdr->yxhr", pooled_q, weights_q, precision=lax.Precision.HIGHEST)
    route_k = jnp.einsum("yxhd,hdr->yxhr", pooled_k, weights_k, precision=lax.Precision.HIGHEST)
    blocks_y, blocks_x = (pooled_q.shape[0], pooled_q.shape[1])
    width = 2 * RADIUS + 1
    shifted = jnp.stack(
        [
            route_k[up : up + blocks_y, left : left + blocks_x]
            for up in range(width)
            for left in range(width)
        ],
        axis=2,
    )
    logits = jnp.einsum(
        "yxhr,yxohr->yxho", route_q, shifted, precision=lax.Precision.HIGHEST
    ) / math.sqrt(RW)
    logits = jnp.where(live[:, :, None, :] > 0, logits, -1e30)
    top = jnp.max(logits, axis=-1, keepdims=True)
    logz = top + jnp.log(jnp.sum(jnp.exp(logits - top), axis=-1, keepdims=True))
    logp = logits - logz
    picks = (chosen[..., None] == jnp.arange(NOFF, dtype=jnp.int32)).astype(jnp.float32)
    return -jnp.sum(picks * logp[:, :, :, None, :])


def per_device(queries, keys, values, pattern, targets, router_q, router_k):
    rim = RADIUS * BS
    stacked = jnp.stack([keys, values])
    extended = extended_2(stacked, (("py", 2), ("px", 3)), rim)
    key_ext = extended[0, 0]
    value_ext = extended[1, 0]
    attended = attend(queries[0], key_ext, value_ext, pattern[0])[None]
    pooled_q = pooling(queries[0])
    pooled_k = pooling(key_ext)
    blocks_y = pooled_q.shape[0]
    blocks_x = pooled_q.shape[1]
    normal = float(TOPK * HEADS * blocks_y * lax.axis_size("py") * blocks_x * lax.axis_size("px"))

    def local_loss(weights_q, weights_k):
        return (
            router_loss(weights_q, weights_k, pooled_q, pooled_k, pattern[0], targets[0]) / normal
        )

    grad_q, grad_k = jax.grad(local_loss, argnums=(0, 1))(router_q, router_k)
    grad_q, grad_k = lax.psum((grad_q, grad_k), ("img", "py", "px"))
    return (attended, grad_q, grad_k)


def solution(mesh):
    return jax.shard_map(
        per_device,
        mesh=mesh,
        in_specs=(
            P("img", "py", "px", None),
            P("img", "py", "px", None),
            P("img", "py", "px", None),
            P("img", "py", "px", None),
            P("img", "py", "px", None, None),
            P(),
            P(),
        ),
        out_specs=(P("img", "py", "px", None), P(), P()),
        check_vma=False,
    )
```

profile of v0, /device:TPU:0, one launch (start us, length us, event | category | flops | bytes accessed | tf_op | source)
XLA Modules:
  0.0 229.2 jit_solution(3661526559126762487)
XLA Ops:
  13.1 4.4 %collective-permute-done.1 = bf16[2,1,8,16,1536]{4,3,2,1,0:T(8,128)(2,1)S(1)} collective-permute-done((bf16[2,1,8,16,1536]{4,3,2,1,0:T(8,128)(2,1)S(1)}, bf16[2,1,8,16,1536]{4,3,2,1,0:T(8,128)(2,1)S(1)}, u32[]{:S(2)}, u32[]{:S(2)}) %collective-permute-start.1) | collective-permute-done | bytes 786464 | tf_op jit(solution)/shard_map/ppermute | solution.py:27
  20.8 4.7 %collective-permute-start.2 = (bf16[2,1,32,8,1536]{4,3,2,1,0:T(8,128)(2,1)}, bf16[2,1,32,8,1536]{4,3,2,1,0:T(8,128)(2,1)}, u32[]{:S(2)}, u32[]{:S(2)}) collective-permute-start(bf16[2,1,32,8,1536]{4,3,2,1,0:T(8,128)(2,1)} %get-tuple-element.121), channel_id=1, source_target_pairs={{0,1},{1,2},{2,3},{4,5},{5,6},{6,7},{8,9},{9,10},{10,11},{12,13},{... | collective-permute-start | bytes 4718600 | tf_op jit(solution)/shard_map/ppermute | solution.py:25
  30.1 20.1 %collective-permute-done.2 = bf16[2,1,32,8,1536]{4,3,2,1,0:T(8,128)(2,1)} collective-permute-done((bf16[2,1,32,8,1536]{4,3,2,1,0:T(8,128)(2,1)}, bf16[2,1,32,8,1536]{4,3,2,1,0:T(8,128)(2,1)}, u32[]{:S(2)}, u32[]{:S(2)}) %collective-permute-start.2) | collective-permute-done | bytes 1572896 | tf_op jit(solution)/shard_map/ppermute | solution.py:25
  50.2 5.8 %collective-permute-done.3 = bf16[2,1,32,8,1536]{4,3,2,1,0:T(8,128)(2,1)} collective-permute-done((bf16[2,1,32,8,1536]{4,3,2,1,0:T(8,128)(2,1)}, bf16[2,1,32,8,1536]{4,3,2,1,0:T(8,128)(2,1)}, u32[]{:S(2)}, u32[]{:S(2)}) %collective-permute-start.3) | collective-permute-done | bytes 1572896 | tf_op jit(solution)/shard_map/ppermute | solution.py:27
  56.1 3.2 %pad_maximum_fusion = bf16[2,1,32,32,1536]{4,3,2,1,0:T(8,128)(2,1)S(1)} fusion(bf16[2,1,32,8,1536]{4,3,2,1,0:T(8,128)(2,1)} %collective-permute-done.3, bf16[2,1,8,16,1536]{4,3,2,1,0:T(8,128)(2,1)} %copy-done.6, bf16[1,1,16,16,1536]{4,3,2,1,0:T(8,128)(2,1)S(1)} %bitcast.152, bf16[1,1,16,16,1536]{4,3,2,1,0:T(8,128)(2,1)S(1)} %bitcast.149, ...), kind=kLoop, calls=%fused_computation.26 | loop fusion | flops 37748736 | bytes 12582912 | tf_op jit(solution)/shard_map/concatenate | solution.py:23
  80.1 2.6 %convolution_bitcast_fusion.1 = f32[12,128,64]{1,2,0:T(8,128)} fusion(f32[2,2,12,64]{3,1,0,2:T(2,128)} %get-tuple-element.126, f32[2,2,12,64]{3,1,0,2:T(2,128)} %get-tuple-element.127, f32[2,2,12,64]{3,1,0,2:T(2,128)} %get-tuple-element.128, f32[2,2,12,64]{3,1,0,2:T(2,128)} %get-tuple-element.129, f32[2,2,12,64]{3,1,0,2:T(2,128)} %get-tuple-element.130, ...), kind=kOutput, calls=%fused_computation.34 | convolution fusion | flops 18972672 | bytes 602112 | tf_op jit(solution)/shard_map/transpose(jvp(yxhd,hdr->yxhr))/dot_general | solution.py:92
  82.7 122.5 %while.12 = (s32[]{:T(128)}, bf16[4,8,8,1536]{3,2,1,0:T(8,128)(2,1)}, s32[4]{0:T(128)S(1)}, bf16[32,32,1536]{2,1,0:T(8,128)(2,1)}, s32[2,2,9]{2,1,0:T(2,128)S(1)...) while((s32[]{:T(128)}, ...), condition=%wide.region_3.4_spmd, body=%wide.region_0.3_spmd.sunk | while | flops 343820224 | bytes 57812960 | solution.py:76
  86.1 3.0 %constant_dynamic-slice_fusion.6 = (bf16[24,24,1536]{2,1,0:T(8,128)(2,1)S(1)}, bf16[24,24,1536]{2,1,0:T(8,128)(2,1)}) fusion(bf16[32,32,1536]{2,1,0:T(8,128)(2,1)S(1)} %get-tuple-element.215, s32[]{:T(128)S(6)} %select_n.109, s32[]{:T(128)S(6)} %select_n.111, bf16[32,32,1536]{2,1,0:T(8,128)(2,1)} %get-tuple-element.212), kind=kLoop, calls=%fused_computation.17.clone.1 | loop fusion | bytes 7077896 | tf_op jit(solution)/shard_map/while/body/eval_jaxpr/dynamic_slice | solution.py:59
  90.6 3.0 %reshape.102 = bf16[576,12,128]{2,1,0:T(8,128)(2,1)S(1)} reshape(bf16[3,3,8,8,1536]{4,3,2,1,0:T(8,128)(2,1)} %copy.118) | data formatting | bytes 3538944 | tf_op jit(solution)/shard_map/while/body/eval_jaxpr/reshape | solution.py:47
  100.8 2.7 %reshape.101 = bf16[576,12,128]{2,1,0:T(8,128)(2,1)} reshape(bf16[3,3,8,8,1536]{4,3,2,1,0:T(8,128)(2,1)S(1)} %copy.117) | data formatting | bytes 3538944 | tf_op jit(solution)/shard_map/while/body/eval_jaxpr/reshape | solution.py:47
  103.5 4.7 %fusion.102 = bf16[64,12,128]{2,0,1:T(8,128)(2,1)} fusion(bf16[576,12,128]{2,1,0:T(8,128)(2,1)} %reshape.101, f32[12,64]{1,0:T(8,128)} %fusion.100, f32[12,64,576]{2,1,0:T(8,128)} %fusion.101, pred[576]{0:T(1024)(128)(4,1)S(1)} %gt.36), kind=kOutput, calls=%fused_computation.10.clone.1 | convolution fusion | flops 115557696 | bytes 3739200 | tf_op jit(solution)/shard_map/while/body/eval_jaxpr/hqk,khd->qhd/dot_general | solution.py:73
  116.7 3.1 %constant_dynamic-slice_fusion.6 = (bf16[24,24,1536]{2,1,0:T(8,128)(2,1)S(1)}, bf16[24,24,1536]{2,1,0:T(8,128)(2,1)}) fusion(bf16[32,32,1536]{2,1,0:T(8,128)(2,1)S(1)} %get-tuple-element.215, s32[]{:T(128)S(6)} %select_n.109, s32[]{:T(128)S(6)} %select_n.111, bf16[32,32,1536]{2,1,0:T(8,128)(2,1)} %get-tuple-element.212), kind=kLoop, calls=%fused_computation.17.clone.1 | loop fusion | bytes 7077896 | tf_op jit(solution)/shard_map/while/body/eval_jaxpr/dynamic_slice | solution.py:59
  121.2 3.0 %reshape.102 = bf16[576,12,128]{2,1,0:T(8,128)(2,1)S(1)} reshape(bf16[3,3,8,8,1536]{4,3,2,1,0:T(8,128)(2,1)} %copy.118) | data formatting | bytes 3538944 | tf_op jit(solution)/shard_map/while/body/eval_jaxpr/reshape | solution.py:47
  131.5 2.7 %reshape.101 = bf16[576,12,128]{2,1,0:T(8,128)(2,1)} reshape(bf16[3,3,8,8,1536]{4,3,2,1,0:T(8,128)(2,1)S(1)} %copy.117) | data formatting | bytes 3538944 | tf_op jit(solution)/shard_map/while/body/eval_jaxpr/reshape | solution.py:47
  134.1 4.7 %fusion.102 = bf16[64,12,128]{2,0,1:T(8,128)(2,1)} fusion(bf16[576,12,128]{2,1,0:T(8,128)(2,1)} %reshape.101, f32[12,64]{1,0:T(8,128)} %fusion.100, f32[12,64,576]{2,1,0:T(8,128)} %fusion.101, pred[576]{0:T(1024)(128)(4,1)S(1)} %gt.36), kind=kOutput, calls=%fused_computation.10.clone.1 | convolution fusion | flops 115557696 | bytes 3739200 | tf_op jit(solution)/shard_map/while/body/eval_jaxpr/hqk,khd->qhd/dot_general | solution.py:73
  147.3 3.0 %constant_dynamic-slice_fusion.6 = (bf16[24,24,1536]{2,1,0:T(8,128)(2,1)S(1)}, bf16[24,24,1536]{2,1,0:T(8,128)(2,1)}) fusion(bf16[32,32,1536]{2,1,0:T(8,128)(2,1)S(1)} %get-tuple-element.215, s32[]{:T(128)S(6)} %select_n.109, s32[]{:T(128)S(6)} %select_n.111, bf16[32,32,1536]{2,1,0:T(8,128)(2,1)} %get-tuple-element.212), kind=kLoop, calls=%fused_computation.17.clone.1 | loop fusion | bytes 7077896 | tf_op jit(solution)/shard_map/while/body/eval_jaxpr/dynamic_slice | solution.py:59
  151.8 3.0 %reshape.102 = bf16[576,12,128]{2,1,0:T(8,128)(2,1)S(1)} reshape(bf16[3,3,8,8,1536]{4,3,2,1,0:T(8,128)(2,1)} %copy.118) | data formatting | bytes 3538944 | tf_op jit(solution)/shard_map/while/body/eval_jaxpr/reshape | solution.py:47
  162.1 2.7 %reshape.101 = bf16[576,12,128]{2,1,0:T(8,128)(2,1)} reshape(bf16[3,3,8,8,1536]{4,3,2,1,0:T(8,128)(2,1)S(1)} %copy.117) | data formatting | bytes 3538944 | tf_op jit(solution)/shard_map/while/body/eval_jaxpr/reshape | solution.py:47
  164.7 4.7 %fusion.102 = bf16[64,12,128]{2,0,1:T(8,128)(2,1)} fusion(bf16[576,12,128]{2,1,0:T(8,128)(2,1)} %reshape.101, f32[12,64]{1,0:T(8,128)} %fusion.100, f32[12,64,576]{2,1,0:T(8,128)} %fusion.101, pred[576]{0:T(1024)(128)(4,1)S(1)} %gt.36), kind=kOutput, calls=%fused_computation.10.clone.1 | convolution fusion | flops 115557696 | bytes 3739200 | tf_op jit(solution)/shard_map/while/body/eval_jaxpr/hqk,khd->qhd/dot_general | solution.py:73
  178.0 3.0 %constant_dynamic-slice_fusion.6 = (bf16[24,24,1536]{2,1,0:T(8,128)(2,1)S(1)}, bf16[24,24,1536]{2,1,0:T(8,128)(2,1)}) fusion(bf16[32,32,1536]{2,1,0:T(8,128)(2,1)S(1)} %get-tuple-element.215, s32[]{:T(128)S(6)} %select_n.109, s32[]{:T(128)S(6)} %select_n.111, bf16[32,32,1536]{2,1,0:T(8,128)(2,1)} %get-tuple-element.212), kind=kLoop, calls=%fused_computation.17.clone.1 | loop fusion | bytes 7077896 | tf_op jit(solution)/shard_map/while/body/eval_jaxpr/dynamic_slice | solution.py:59
  182.5 3.0 %reshape.102 = bf16[576,12,128]{2,1,0:T(8,128)(2,1)S(1)} reshape(bf16[3,3,8,8,1536]{4,3,2,1,0:T(8,128)(2,1)} %copy.118) | data formatting | bytes 3538944 | tf_op jit(solution)/shard_map/while/body/eval_jaxpr/reshape | solution.py:47
  192.7 2.7 %reshape.101 = bf16[576,12,128]{2,1,0:T(8,128)(2,1)} reshape(bf16[3,3,8,8,1536]{4,3,2,1,0:T(8,128)(2,1)S(1)} %copy.117) | data formatting | bytes 3538944 | tf_op jit(solution)/shard_map/while/body/eval_jaxpr/reshape | solution.py:47
  195.4 4.7 %fusion.102 = bf16[64,12,128]{2,0,1:T(8,128)(2,1)} fusion(bf16[576,12,128]{2,1,0:T(8,128)(2,1)} %reshape.101, f32[12,64]{1,0:T(8,128)} %fusion.100, f32[12,64,576]{2,1,0:T(8,128)} %fusion.101, pred[576]{0:T(1024)(128)(4,1)S(1)} %gt.36), kind=kOutput, calls=%fused_computation.10.clone.1 | convolution fusion | flops 115557696 | bytes 3739200 | tf_op jit(solution)/shard_map/while/body/eval_jaxpr/hqk,khd->qhd/dot_general | solution.py:73
  207.3 11.4 %all-reduce.12.cloned.1.call-done = (f32[12,128,64]{1,2,0:T(8,128)}, f32[12,128,64]{1,2,0:T(8,128)}) async-done(((f32[12,128,64]{1,2,0:T(8,128)}, f32[12,128,64]{1,2,0:T(8,128)}), (f32[12,128,64]{1,2,0:T(8,128)}, f32[12,128,64]{1,2,0:T(8,128)})) %all-reduce.12.cloned.1.call-update) | async-done | bytes 786448 | tf_op jit(solution)/shard_map/psum | solution.py:133
  (135 shorter events, 98.0 us)
Async XLA Ops:
  7.2 55.7 %copy-start = (f32[12,128,64]{1,2,0:T(8,128)S(1)}, f32[12,128,64]{1,2,0:T(8,128)}, u32[]{:S(2)}) copy-start(f32[12,128,64]{1,2,0:T(8,128)} %param.15) | copy-start | bytes 1179652
  7.2 11.2 %copy-start.3 = (bf16[1,16,16,1536]{3,2,1,0:T(8,128)(2,1)S(1)}, bf16[1,16,16,1536]{3,2,1,0:T(8,128)(2,1)}, u32[]{:S(2)}) copy-start(bf16[1,16,16,1536]{3,2,1,0:T(8,128)(2,1)} %param.10) | copy-start | bytes 2359300
  7.2 11.2 %copy-start.4 = (bf16[1,16,16,1536]{3,2,1,0:T(8,128)(2,1)S(1)}, bf16[1,16,16,1536]{3,2,1,0:T(8,128)(2,1)}, u32[]{:S(2)}) copy-start(bf16[1,16,16,1536]{3,2,1,0:T(8,128)(2,1)} %param.11) | copy-start | bytes 2359300
  7.2 211.6 %all-reduce.12.cloned.1.call-start = ((), (), s32[]{:S(2)}) async-start(), calls=%async_computation | async-start | bytes 1572864 | tf_op jit(solution)/shard_map/psum | solution.py:133
  8.9 4.3 %collective-permute-start = (bf16[2,1,8,16,1536]{4,3,2,1,0:T(8,128)(2,1)S(1)}, bf16[2,1,8,16,1536]{4,3,2,1,0:T(8,128)(2,1)S(1)}, u32[]{:S(2)}, u32[]{:S(2)}) collective-permute-start(bf16[2,1,8,16,1536]{4,3,2,1,0:T(8,128)(2,1)S(1)} %get-tuple-element.123), channel_id=1, source_target_pairs={{0,4},{4,8},{8,12},{1,5},{5,9},{9,13},{2,6},{6,10},{10,14},{3,7},{... | collective-permute-start | bytes 2359304 | tf_op jit(solution)/shard_map/ppermute | solution.py:25
  11.3 6.3 %collective-permute-start.1 = (bf16[2,1,8,16,1536]{4,3,2,1,0:T(8,128)(2,1)S(1)}, bf16[2,1,8,16,1536]{4,3,2,1,0:T(8,128)(2,1)S(1)}, u32[]{:S(2)}, u32[]{:S(2)}) collective-permute-start(bf16[2,1,8,16,1536]{4,3,2,1,0:T(8,128)(2,1)S(1)} %get-tuple-element.124), channel_id=1, source_target_pairs={{4,0},{8,4},{12,8},{5,1},{9,5},{13,9},{6,2},{10,6},{14,10},{7,3},{... | collective-permute-start | bytes 2359304 | tf_op jit(solution)/shard_map/ppermute | solution.py:27
  17.5 0.9 copy-start.6
  18.9 7.9 %copy-start.11 = (s32[1,2,2,9]{3,2,1,0:T(2,128)S(1)}, s32[1,2,2,9]{3,2,1,0:T(2,128)}, u32[]{:S(2)}) copy-start(s32[1,2,2,9]{3,2,1,0:T(2,128)} %param.12) | copy-start | bytes 436
  18.9 9.4 %copy-start.5 = (bf16[1,16,16,1536]{3,2,1,0:T(8,128)(2,1)S(1)}, bf16[1,16,16,1536]{3,2,1,0:T(8,128)(2,1)}, u32[]{:S(2)}) copy-start(bf16[1,16,16,1536]{3,2,1,0:T(8,128)(2,1)} %param.9) | copy-start | bytes 2359300
  20.8 29.4 %collective-permute-start.2 = (bf16[2,1,32,8,1536]{4,3,2,1,0:T(8,128)(2,1)}, bf16[2,1,32,8,1536]{4,3,2,1,0:T(8,128)(2,1)}, u32[]{:S(2)}, u32[]{:S(2)}) collective-permute-start(bf16[2,1,32,8,1536]{4,3,2,1,0:T(8,128)(2,1)} %get-tuple-element.121), channel_id=1, source_target_pairs={{0,1},{1,2},{2,3},{4,5},{5,6},{6,7},{8,9},{9,10},{10,11},{12,13},{... | collective-permute-start | bytes 4718600 | tf_op jit(solution)/shard_map/ppermute | solution.py:25
  25.4 30.6 %collective-permute-start.3 = (bf16[2,1,32,8,1536]{4,3,2,1,0:T(8,128)(2,1)}, bf16[2,1,32,8,1536]{4,3,2,1,0:T(8,128)(2,1)}, u32[]{:S(2)}, u32[]{:S(2)}) collective-permute-start(bf16[2,1,32,8,1536]{4,3,2,1,0:T(8,128)(2,1)} %get-tuple-element.122), channel_id=1, source_target_pairs={{1,0},{2,1},{3,2},{5,4},{6,5},{7,6},{9,8},{10,9},{11,10},{13,12},{... | collective-permute-start | bytes 4718600 | tf_op jit(solution)/shard_map/ppermute | solution.py:27
  28.4 27.7 %copy-start.10 = (f32[2,2,12,128]{3,2,1,0:T(8,128)}, f32[2,2,12,128]{3,2,1,0:T(8,128)S(1)}, u32[]{:S(2)}) copy-start(f32[2,2,12,128]{3,2,1,0:T(8,128)S(1)} %broadcast_multiply_fusion.1) | copy-start | bytes 73732
  30.1 33.8 %copy-start.9 = (f32[12,2,2,64]{3,2,1,0:T(2,128)}, f32[12,2,2,64]{3,2,1,0:T(2,128)S(1)}, u32[]{:S(2)}) copy-start(f32[12,2,2,64]{3,2,1,0:T(2,128)S(1)} %fusion.37) | copy-start | bytes 36868
  62.3 0.7 copy-start.8
  63.9 0.7 copy-start.7
  82.7 6.4 %copy-start.1 = (bf16[32,32,1536]{2,1,0:T(8,128)(2,1)}, bf16[32,32,1536]{2,1,0:T(8,128)(2,1)S(1)}, u32[]{:S(2)}) copy-start(bf16[32,32,1536]{2,1,0:T(8,128)(2,1)S(1)} %get-tuple-element.215) | copy-start | bytes 9437188 | tf_op jit(solution)/shard_map/while
  103.5 9.9 %copy-start.2 = (bf16[32,32,1536]{2,1,0:T(8,128)(2,1)S(1)}, bf16[32,32,1536]{2,1,0:T(8,128)(2,1)}, u32[]{:S(2)}) copy-start(bf16[32,32,1536]{2,1,0:T(8,128)(2,1)} %copy-done.1) | copy-start | bytes 9437188 | tf_op jit(solution)/shard_map/while
  113.4 6.4 %copy-start.1 = (bf16[32,32,1536]{2,1,0:T(8,128)(2,1)}, bf16[32,32,1536]{2,1,0:T(8,128)(2,1)S(1)}, u32[]{:S(2)}) copy-start(bf16[32,32,1536]{2,1,0:T(8,128)(2,1)S(1)} %get-tuple-element.215) | copy-start | bytes 9437188 | tf_op jit(solution)/shard_map/while
  134.1 9.9 %copy-start.2 = (bf16[32,32,1536]{2,1,0:T(8,128)(2,1)S(1)}, bf16[32,32,1536]{2,1,0:T(8,128)(2,1)}, u32[]{:S(2)}) copy-start(bf16[32,32,1536]{2,1,0:T(8,128)(2,1)} %copy-done.1) | copy-start | bytes 9437188 | tf_op jit(solution)/shard_map/while
  144.0 6.4 %copy-start.1 = (bf16[32,32,1536]{2,1,0:T(8,128)(2,1)}, bf16[32,32,1536]{2,1,0:T(8,128)(2,1)S(1)}, u32[]{:S(2)}) copy-start(bf16[32,32,1536]{2,1,0:T(8,128)(2,1)S(1)} %get-tuple-element.215) | copy-start | bytes 9437188 | tf_op jit(solution)/shard_map/while
  164.7 9.9 %copy-start.2 = (bf16[32,32,1536]{2,1,0:T(8,128)(2,1)S(1)}, bf16[32,32,1536]{2,1,0:T(8,128)(2,1)}, u32[]{:S(2)}) copy-start(bf16[32,32,1536]{2,1,0:T(8,128)(2,1)} %copy-done.1) | copy-start | bytes 9437188 | tf_op jit(solution)/shard_map/while
  174.6 6.4 %copy-start.1 = (bf16[32,32,1536]{2,1,0:T(8,128)(2,1)}, bf16[32,32,1536]{2,1,0:T(8,128)(2,1)S(1)}, u32[]{:S(2)}) copy-start(bf16[32,32,1536]{2,1,0:T(8,128)(2,1)S(1)} %get-tuple-element.215) | copy-start | bytes 9437188 | tf_op jit(solution)/shard_map/while
  195.4 9.9 %copy-start.2 = (bf16[32,32,1536]{2,1,0:T(8,128)(2,1)S(1)}, bf16[32,32,1536]{2,1,0:T(8,128)(2,1)}, u32[]{:S(2)}) copy-start(bf16[32,32,1536]{2,1,0:T(8,128)(2,1)} %copy-done.1) | copy-start | bytes 9437188 | tf_op jit(solution)/shard_map/while
Sparse Core Ops, SparseCore 0:
  82.8 135.8 all-reduce.11
where the time goes:
time: 231 us; the launch traced here: 229 us
  local copies, waits for them, and re-layouts  93.3 us (40%)
  matrix products  46.1 us (20%)
  waiting for transfers between devices  42.3 us (18%)
  between operations  14.3 us (6%)
  other arithmetic  12.5 us (5%)
  loops' own time  10.9 us (5%)
  starting transfers between devices  9.67 us (4%)
    reshape x8, local copies, waits for them, and re-layouts, regroup(): return window.reshape(width, BS, width, BS, feat).transpose(0, 2, 1, 3, 4...  22.8 us
    ppermute x2, waiting for transfers between devices, extended_2(): lax.ppermute(tail, axis, [(i, (i + 1) % count) for i in range(ends)])  20.6 us
    dot_general x4, matrix products, one_block(): jnp.einsum('hqk,khd->qhd', probs, window_v, preferred_element_type=jnp.fl...  18.8 us
    transpose x8, local copies, waits for them, and re-layouts, regroup(): return window.reshape(width, BS, width, BS, feat).transpose(0, 2, 1, 3, 4...  12.4 us
    dynamic_slice x4, local copies, waits for them, and re-layouts, one_block(): lax.dynamic_slice(key_ext, (start_y, start_x, anchor), (side, side, feat))  12.2 us
    psum x1, waiting for transfers between devices, per_device(): grad_q, grad_k = lax.psum((grad_q, grad_k), ('img', 'py', 'px'))  11.4 us
    another operation x1, loops' own time, attend(): outs = lax.map(one_block, jnp.arange(blocks_y * blocks_x, dtype=jnp.int32))  10.9 us
    ppermute x2, waiting for transfers between devices, extended_2(): lax.ppermute(head, axis, [((i + 1) % count, i) for i in range(ends)])  10.3 us
  transfers between devices with their start and end apart: 5, of which 5 were waited for; matrix products, arithmetic and copies ran while one was open for 51% of the time, Pallas kernels for 0%

commit v1 on v0

v1 whole, which is shorter than its diff:
```python
import functools
import math

import jax
import jax.numpy as jnp
from jax import lax
from jax.experimental import pallas as pl
from jax.experimental.pallas import tpu as pltpu
from jax.sharding import PartitionSpec as P

HEADS = 12
DH = 128
RW = 64
BS = 8
TOPK = 3
NOFF = 9
HG = 2
NG = HEADS // HG
GL = HG * DH
WINDOW = 3
BB = BS * BS
DEAD = -1e30
LIVE = 3e38
MESH = pl.DeviceIdType.MESH
F32 = jnp.float32
BF16 = jnp.bfloat16
HIGH = lax.Precision.HIGHEST


def lanes(start, size):
    return pl.ds(pl.multiple_of(start, DH), size)


def tile_blocks(x):
    return [x[by * BS:(by + 1) * BS, bx * BS:(bx + 1) * BS] for by in range(2) for bx in range(2)]


def dot_t(a, b):
    return lax.dot_general(a, b, (((1,), (1,)), ((), ())), preferred_element_type=F32)


def kernel(
    sizes, q_ref, k_ref, v_ref, pat_ref, tgt_ref, wq_ref, wk_ref,
    out_ref, gq_ref, gk_ref,
    q_s, zs, zr, yr, cr, acc, den, top, cap_a, cap_b, msg, pool, xbuf, gbuf,
    zs_sem, zr_sem, ys_sem, yr_sem, cs_sem, cr_sem,
    ms_sem, mr_sem, xs_sem, xr_sem, gs_sem, gr_sem, hs_sem, hr_sem,
):
    ni, npy, npx = sizes
    per_py = HEADS // npy
    group = npy * npx
    img = lax.axis_index("img")
    py = lax.axis_index("py")
    px = lax.axis_index("px")
    me = py * npx + px
    has_x = (px > 0, px < npx - 1)
    has_y = (py > 0, py < npy - 1)
    to_x = (px - 1, px + 1)
    to_y = (py - 1, py + 1)

    barrier = pltpu.get_barrier_semaphore()
    for d in range(1, group):
        other = lax.rem(me + d, group)
        pl.semaphore_signal(
            barrier, inc=1,
            device_id={"py": lax.div(other, npx), "px": lax.rem(other, npx)},
            device_id_type=MESH,
        )
    for d in range(1, ni):
        pl.semaphore_signal(
            barrier, inc=1, device_id={"img": lax.rem(img + d, ni)}, device_id_type=MESH
        )

    def z_copy(side, g):
        return pltpu.make_async_remote_copy(
            src_ref=zs.at[side, g], dst_ref=zr.at[1 - side, g],
            send_sem=zs_sem.at[side, g], recv_sem=zr_sem.at[1 - side, g],
            device_id={"px": to_x[side]}, device_id_type=MESH,
        )

    def z_arrival(side, g):
        return pltpu.make_async_remote_copy(
            src_ref=zs.at[side, g], dst_ref=zr.at[side, g],
            send_sem=zs_sem.at[side, g], recv_sem=zr_sem.at[side, g],
            device_id={"px": to_x[side]}, device_id_type=MESH,
        )

    def y_rows(which, side, g):
        ref = (k_ref, v_ref)[which]
        return ref.at[pl.ds(side * BS, BS), :, lanes(g * GL, GL)]

    def y_copy(which, side, g, slot):
        return pltpu.make_async_remote_copy(
            src_ref=y_rows(which, side, g), dst_ref=yr.at[slot, g, which],
            send_sem=ys_sem.at[side, which, g], recv_sem=yr_sem.at[slot, which, g],
            device_id={"py": to_y[side]}, device_id_type=MESH,
        )

    def c_copy(side_y, side_x, g, slot):
        return pltpu.make_async_remote_copy(
            src_ref=zr.at[side_x, g, :, pl.ds(side_y * BB, BB)],
            dst_ref=cr.at[slot, side_x, g],
            send_sem=cs_sem.at[side_y, side_x, g], recv_sem=cr_sem.at[slot, side_x, g],
            device_id={"py": to_y[side_y]}, device_id_type=MESH,
        )

    def send_z(g):
        for side in range(2):
            @pl.when(has_x[side])
            def _():
                z_copy(side, g).start()

    def send_y(g):
        for side in range(2):
            @pl.when(has_y[side])
            def _():
                for which in range(2):
                    y_copy(which, side, g, 1 - side).start()

    def cap_of(block, dy, dx):
        by, bx = divmod(block, 2)
        off = (dy + 1) * 3 + dx + 1
        return jnp.where(pat_ref[0, by, bx, off] > 0, F32(LIVE), F32(DEAD))

    lane_a = lax.broadcasted_iota(jnp.int32, (BS, 4 * BB), 1)
    lane_b = lax.broadcasted_iota(jnp.int32, (BS, 2 * BB), 1)
    for block in range(4):
        by, bx = divmod(block, 2)
        sy, sx = 2 * by - 1, 2 * bx - 1
        col_a = lax.rem(lax.div(lane_a, BS), 2)
        col_b = lax.rem(lax.div(lane_b, BS), 2)

        def pick(row, col, a, b):
            return jnp.where(col > 0, b, a)

        rows = [
            jnp.where(col_a > 0, cap_of(block, r - by, 1 - bx), cap_of(block, r - by, -bx))
            for r in range(2)
        ]
        cap_a[block] = jnp.where(lane_a >= 2 * BB, rows[1], rows[0])
        cap_b[block, :, 0:128] = jnp.where(
            lane_b >= BB, cap_of(block, 1 - by, sx), cap_of(block, -by, sx)
        )
        cap_b[block, :, 128:256] = jnp.where(
            col_b > 0, cap_of(block, sy, 1 - bx), cap_of(block, sy, -bx)
        )
        corner = cap_of(block, sy, sx)
        if bx == 0:
            cap_b[block, :, 256:384] = jnp.where(lane_b >= BB, F32(DEAD), corner)
        else:
            cap_b[block, :, 256:384] = jnp.where(lane_b >= BB, corner, F32(DEAD))

    def prepare(g, carry):
        for j in range(HG):
            h = g * HG + j
            hl = lanes(h * DH, DH)
            jl = pl.ds(j * DH, DH)
            q = q_ref[:, :, hl].astype(F32)
            k = k_ref[:, :, hl].astype(F32)
            v = v_ref[:, :, hl].astype(F32)
            parts = tile_blocks(q)
            q_s[h] = jnp.concatenate([b.reshape(BB, DH) for b in parts], axis=0).astype(BF16)
            for b in range(4):
                msg[h, b:b + 1, :] = jnp.sum(
                    jnp.sum(parts[b], axis=0), axis=0, keepdims=True) / BB
            parts = tile_blocks(k)
            for b in range(4):
                msg[h, 4 + b:5 + b, :] = jnp.sum(
                    jnp.sum(parts[b], axis=0), axis=0, keepdims=True) / BB
            for side in range(2):
                sl = slice(side * BS, (side + 1) * BS)
                zs[side, g, 0, :, jl] = k[:, sl, :].reshape(2 * BB, DH).astype(BF16)
                zs[side, g, 1, :, jl] = v[:, sl, :].reshape(2 * BB, DH).astype(BF16)
        return carry

    lax.fori_loop(0, NG, prepare, 0)

    lane = lax.broadcasted_iota(jnp.int32, (1, DH), 1)
    code_rows = []
    for block in range(4):
        by, bx = divmod(block, 2)
        row = jnp.full((1, DH), -1.0, F32)
        for o in range(NOFF):
            row = jnp.where(
                lane == o, jnp.where(pat_ref[0, by, bx, o] > 0, F32(0.0), F32(-1.0)), row)
        code_rows.append(row)

    def encode(h, carry):
        for block in range(4):
            by, bx = divmod(block, 2)
            chosen = lane == tgt_ref[0, by, bx, h, 0]
            for t in range(1, TOPK):
                chosen = chosen | (lane == tgt_ref[0, by, bx, h, t])
            row = jnp.where(code_rows[block] < 0, F32(-1.0), jnp.where(chosen, F32(1.0), F32(0.0)))
            msg[h, 8 + block:9 + block, :] = row
        msg[h, 12:16, :] = jnp.zeros((4, DH), F32)
        return carry

    lax.fori_loop(0, HEADS, encode, 0)

    for side in range(2):
        @pl.when(jnp.logical_not(has_x[side]))
        def _():
            zr[side] = jnp.zeros(zr.shape[1:], BF16)
        @pl.when(jnp.logical_not(has_y[side]))
        def _():
            yr[side] = jnp.zeros(yr.shape[1:], BF16)
        for other in range(2):
            @pl.when(jnp.logical_not(has_y[side] & has_x[other]))
            def _():
                cr[side, other] = jnp.zeros(cr.shape[2:], BF16)

    pl.semaphore_wait(barrier, group - 1 + ni - 1)
    send_z(0)

    def owner_of(h):
        return h // per_py, h % npx

    def m_copy(h, slot):
        oy, ox = owner_of(h)
        return pltpu.make_async_remote_copy(
            src_ref=msg.at[h], dst_ref=pool.at[slot],
            send_sem=ms_sem.at[h], recv_sem=mr_sem.at[slot],
            device_id={"py": oy, "px": ox}, device_id_type=MESH,
        )

    for h in range(HEADS):
        oy, ox = owner_of(h)
        @pl.when(jnp.logical_not((py == oy) & (px == ox)))
        def _():
            m_copy(h, me).start()
    turn = lax.rem(px + npx * HEADS - py * per_py, npx)
    own = turn < per_py
    my_head = jnp.minimum(py * per_py + turn, HEADS - 1)

    send_y(0)
    for g in range(1, WINDOW):
        send_z(g)
        send_y(g)

    scale = math.log2(math.e) / math.sqrt(DH)
    ones = jnp.ones((2 * DH, DH), BF16)

    def local_heads(g, carry):
        for j in range(HG):
            h = g * HG + j
            hl = lanes(h * DH, DH)
            key = k_ref[:, :, hl].reshape(4 * BB, DH)
            val = v_ref[:, :, hl].reshape(4 * BB, DH)
            s = dot_t(q_s[h], key)
            s = jnp.minimum(s.reshape(4, BS, BS, 4 * BB), cap_a[...][:, None]).reshape(4 * BB, 4 * BB)
            m = jnp.max(s, axis=-1, keepdims=True)
            p = jnp.exp2((s - m) * scale).astype(BF16)
            r = jnp.dot(p, jnp.concatenate([val, ones], axis=1), preferred_element_type=F32)
            acc[h] = r[:, :DH]
            den[h] = r[:, DH:]
            top[h] = jnp.broadcast_to(m, (4 * BB, DH))
        return carry

    lax.fori_loop(0, NG // 2, local_heads, 0)

    def x_copy(d):
        return pltpu.make_async_remote_copy(
            src_ref=xbuf.at[img], dst_ref=xbuf.at[img],
            send_sem=xs_sem.at[d], recv_sem=xr_sem.at[d],
            device_id={"img": lax.rem(img + d, ni)}, device_id_type=MESH,
        )

    def x_arrival(d):
        src = lax.rem(img + ni - d, ni)
        return pltpu.make_async_remote_copy(
            src_ref=xbuf.at[src], dst_ref=xbuf.at[src],
            send_sem=xs_sem.at[d], recv_sem=xr_sem.at[d],
            device_id={"img": lax.rem(img + d, ni)}, device_id_type=MESH,
        )

    @pl.when(own)
    def _():
        pool[me] = msg[my_head]
        for src in range(group):
            @pl.when(me != src)
            def _():
                m_copy(0, src).wait_recv()
        nb = 4 * group
        pq = pool[:, 0:4, :].reshape(nb, DH) if False else jnp.concatenate(
            [pool[s, 0:4, :] for s in range(group)], axis=0)
        pk = jnp.concatenate([pool[s, 4:8, :] for s in range(group)], axis=0)
        code = jnp.concatenate([pool[s, 8:12, :] for s in range(group)], axis=0)
        wq = wq_ref[my_head]
        wk = wk_ref[my_head]
        rq = jnp.dot(pq, wq, precision=HIGH, preferred_element_type=F32)
        rk = jnp.dot(pk, wk, precision=HIGH, preferred_element_type=F32)
        logits = lax.dot_general(
            rq, rk, (((1,), (1,)), ((), ())), precision=HIGH, preferred_element_type=F32
        ) / math.sqrt(RW)

        def place(i):
            s = lax.div(i, 4)
            b = lax.rem(i, 4)
            return (
                lax.div(s, npx) * 2 + lax.div(b, 2),
                lax.rem(s, npx) * 2 + lax.rem(b, 2),
            )

        iy, ix = place(lax.broadcasted_iota(jnp.int32, (nb, nb), 0))
        jy, jx = place(lax.broadcasted_iota(jnp.int32, (nb, nb), 1))
        picks = jnp.full((nb, nb), -1.0, F32)
        for o in range(NOFF):
            dy, dx = o // 3 - 1, o % 3 - 1
            picks = jnp.where((jy - iy == dy) & (jx - ix == dx), code[:, o:o + 1], picks)
        live = picks >= 0
        logits = jnp.where(live, logits, DEAD)
        e = jnp.where(live, jnp.exp(logits - jnp.max(logits, axis=-1, keepdims=True)), 0.0)
        prob = e / jnp.sum(e, axis=-1, keepdims=True)
        picks = jnp.where(live, picks, 0.0)
        count = jnp.sum(picks, axis=-1, keepdims=True)
        normal = float(TOPK * HEADS * nb) * math.sqrt(RW)
        dl = jnp.where(live, count * prob - picks, 0.0) / normal
        drq = jnp.dot(dl, rk, precision=HIGH, preferred_element_type=F32)
        drk = lax.dot_general(
            dl, rq, (((0,), (0,)), ((), ())), precision=HIGH, preferred_element_type=F32)
        grads = [
            lax.dot_general(
                a, b, (((0,), (0,)), ((), ())), precision=HIGH, preferred_element_type=F32)
            for a, b in ((pq, drq), (pk, drk))
        ]
        xbuf[img] = jnp.concatenate(grads, axis=1)
        for d in range(1, ni):
            x_copy(d).start()

    lax.fori_loop(NG // 2, NG, local_heads, 0)

    def g_copy(d, head):
        return pltpu.make_async_remote_copy(
            src_ref=gbuf.at[head], dst_ref=gbuf.at[head],
            send_sem=gs_sem.at[d], recv_sem=gr_sem.at[head],
            device_id={"px": lax.rem(px + d, npx)}, device_id_type=MESH,
        )

    def sum_images():
        @pl.when(own)
        def _():
            for d in range(1, ni):
                x_arrival(d).wait_recv()
            total = xbuf[0]
            for i in range(1, ni):
                total = total + xbuf[i]
            gbuf[my_head] = total.astype(BF16)
            for d in range(1, npx):
                g_copy(d, my_head).start()

    def h_copy(bit, start, count, slot):
        mate = py + bit - 2 * bit * lax.rem(lax.div(py, bit), 2)
        return pltpu.make_async_remote_copy(
            src_ref=gbuf.at[pl.ds(start, count)], dst_ref=gbuf.at[pl.ds(start, count)],
            send_sem=hs_sem.at[slot], recv_sem=hr_sem.at[slot],
            device_id={"py": mate}, device_id_type=MESH,
        )

    bits = []
    b = npy // 2
    while b:
        bits.append(b)
        b //= 2

    def held(step):
        found = [py]
        for s in range(step):
            bit = bits[s]
            found = found + [r + bit - 2 * bit * lax.rem(lax.div(r, bit), 2) for r in found]
        return found

    def slots(step):
        return [2 ** step - 1 + i for i in range(2 ** step)]

    def cube_send(step):
        for r, slot in zip(held(step), slots(step)):
            h_copy(bits[step], r * per_py, per_py, slot).start()

    def cube_wait(step):
        bit = bits[step]
        for r, slot in zip(held(step), slots(step)):
            other = r + bit - 2 * bit * lax.rem(lax.div(r, bit), 2)
            h_copy(bit, other * per_py, per_py, slot).wait_recv()

    def gather_px():
        for i in range(per_py):
            head = py * per_py + i
            @pl.when(jnp.logical_not(own & (my_head == head)))
            def _():
                g_copy(1, head).wait_recv()

    def finish_grads():
        for h in range(HEADS):
            g = gbuf[h].astype(F32)
            gq_ref[h] = g[:, :RW]
            gk_ref[h] = g[:, RW:]

    def rim_heads(g):
        for j in range(HG):
            h = g * HG + j
            jl = pl.ds(j * DH, DH)
            q = q_s[h]
            qb = [q[i * BB:(i + 1) * BB] for i in range(4)]
            sx, sy, vx, vy = [], [], [], []
            for side in range(2):
                key = zr[side, g, 0, :, jl]
                sx.append(dot_t(jnp.concatenate([qb[side], qb[2 + side]], axis=0), key))
                vx.append(jnp.concatenate([zr[side, g, 1, :, jl], ones[:2 * BB]], axis=1))
                key = jnp.concatenate(
                    [yr[side, g, 0, :, :, jl].reshape(2 * BB, DH),
                     cr[side, 0, g, 0, :, jl], cr[side, 1, g, 0, :, jl]], axis=0)
                val = jnp.concatenate(
                    [yr[side, g, 1, :, :, jl].reshape(2 * BB, DH),
                     cr[side, 0, g, 1, :, jl], cr[side, 1, g, 1, :, jl]], axis=0)
                sy.append(dot_t(q[side * 2 * BB:(side + 1) * 2 * BB], key))
                vy.append(jnp.concatenate([val, ones], axis=1))
            wx, wy, ms = [], [], []
            for i in range(4):
                by, bx = divmod(i, 2)
                a = sx[bx][by * BB:(by + 1) * BB].reshape(BS, BS, 2 * BB)
                c = sy[by][bx * BB:(bx + 1) * BB].reshape(BS, BS, 4 * BB)
                a = jnp.minimum(a, cap_b[i, :, 0:2 * BB][None]).reshape(BB, 2 * BB)
                c = jnp.minimum(c, cap_b[i, :, 2 * BB:6 * BB][None]).reshape(BB, 4 * BB)
                widest = jnp.maximum(a, jnp.maximum(c[:, :2 * BB], c[:, 2 * BB:]))
                m = jnp.maximum(
                    top[h, i * BB:(i + 1) * BB, :], jnp.max(widest, axis=-1, keepdims=True))
                wx.append(jnp.exp2((a - m) * scale).astype(BF16))
                wy.append(jnp.exp2((c - jnp.concatenate([m, m], axis=1)) * scale).astype(BF16))
                ms.append(m)
            rx = [
                jnp.dot(jnp.concatenate([wx[s], wx[2 + s]], axis=0), vx[s],
                        preferred_element_type=F32)
                for s in range(2)
            ]
            ry = [
                jnp.dot(jnp.concatenate([wy[2 * s], wy[2 * s + 1]], axis=0), vy[s],
                        preferred_element_type=F32)
                for s in range(2)
            ]
            outs = []
            for i in range(4):
                by, bx = divmod(i, 2)
                rows = slice(i * BB, (i + 1) * BB)
                old = jnp.exp2((top[h, rows, :] - ms[i]) * scale)
                r = rx[bx][by * BB:(by + 1) * BB] + ry[by][bx * BB:(bx + 1) * BB]
                num = acc[h, rows, :] * old + r[:, :DH]
                tot = den[h, rows, :] * old + r[:, DH:]
                outs.append((num / tot).reshape(BS, BS, DH))
            for by in range(2):
                out_ref[by * BS:(by + 1) * BS, :, lanes(h * DH, DH)] = jnp.concatenate(
                    [outs[2 * by], outs[2 * by + 1]], axis=1).astype(BF16)

    def advance(s, carry):
        @pl.when(s < NG)
        def _():
            for side in range(2):
                @pl.when(has_x[side])
                def _():
                    z_arrival(side, s).wait_recv()
                for side_y in range(2):
                    @pl.when(has_x[side] & has_y[side_y])
                    def _():
                        c_copy(side_y, side, s, 1 - side_y).start()

            @pl.when(s + WINDOW < NG)
            def _():
                send_z(s + WINDOW)
                send_y(s + WINDOW)

        @pl.when(s >= 1)
        def _():
            g = s - 1
            for side in range(2):
                @pl.when(has_y[side])
                def _():
                    for which in range(2):
                        y_copy(which, side, g, side).wait_recv()
                for side_x in range(2):
                    @pl.when(has_y[side] & has_x[side_x])
                    def _():
                        c_copy(side, side_x, g, side).wait_recv()
            rim_heads(g)

        @pl.when(s == 0)
        def _():
            sum_images()
        @pl.when(s == 2)
        def _():
            gather_px()
            cube_send(0)
        for step in range(1, len(bits)):
            @pl.when(s == 2 + step)
            def _():
                cube_wait(step - 1)
                cube_send(step)
        @pl.when(s == 2 + len(bits))
        def _():
            cube_wait(len(bits) - 1)
            finish_grads()
        return carry

    lax.fori_loop(0, NG + 1, advance, 0)

    def drain(g, carry):
        for side in range(2):
            @pl.when(has_x[side])
            def _():
                z_copy(side, g).wait_send()
            @pl.when(has_y[side])
            def _():
                for which in range(2):
                    y_copy(which, side, g, 1 - side).wait_send()
            for side_x in range(2):
                @pl.when(has_y[side] & has_x[side_x])
                def _():
                    c_copy(side, side_x, g, 1 - side).wait_send()
        return carry

    lax.fori_loop(0, NG, drain, 0)
    for h in range(HEADS):
        oy, ox = owner_of(h)
        @pl.when(jnp.logical_not((py == oy) & (px == ox)))
        def _():
            m_copy(h, me).wait_send()
    @pl.when(own)
    def _():
        for d in range(1, ni):
            x_copy(d).wait_send()
        for d in range(1, npx):
            g_copy(d, my_head).wait_send()
    for step in range(len(bits)):
        for r, slot in zip(held(step), slots(step)):
            h_copy(bits[step], r * per_py, per_py, slot).wait_send()


def per_device(sizes, queries, keys, values, pattern, targets, router_q, router_k):
    ni, npy, npx = sizes
    _, ty, tx, feat = queries.shape
    group = npy * npx
    dma = pltpu.SemaphoreType.DMA
    vmem = pl.BlockSpec(memory_space=pltpu.VMEM)
    smem = pl.BlockSpec(memory_space=pltpu.SMEM)
    attended, grad_q, grad_k = pl.pallas_call(
        functools.partial(kernel, sizes),
        out_shape=(
            jax.ShapeDtypeStruct((ty, tx, feat), BF16),
            jax.ShapeDtypeStruct((HEADS, DH, RW), F32),
            jax.ShapeDtypeStruct((HEADS, DH, RW), F32),
        ),
        in_specs=[vmem, vmem, vmem, smem, smem, vmem, vmem],
        out_specs=(vmem, vmem, vmem),
        scratch_shapes=[
            pltpu.VMEM((HEADS, 4 * BB, DH), BF16),
            pltpu.VMEM((2, NG, 2, 2 * BB, GL), BF16),
            pltpu.VMEM((2, NG, 2, 2 * BB, GL), BF16),
            pltpu.VMEM((2, NG, 2, BS, 2 * BS, GL), BF16),
            pltpu.VMEM((2, 2, NG, 2, BB, GL), BF16),
            pltpu.VMEM((HEADS, 4 * BB, DH), F32),
            pltpu.VMEM((HEADS, 4 * BB, DH), F32),
            pltpu.VMEM((HEADS, 4 * BB, DH), F32),
            pltpu.VMEM((4, BS, 4 * BB), F32),
            pltpu.VMEM((4, BS, 6 * BB), F32),
            pltpu.VMEM((HEADS, 16, DH), F32),
            pltpu.VMEM((group, 16, DH), F32),
            pltpu.VMEM((ni, DH, 2 * RW), F32),
            pltpu.VMEM((HEADS, DH, 2 * RW), BF16),
            dma((2, NG)), dma((2, NG)),
            dma((2, 2, NG)), dma((2, 2, NG)),
            dma((2, 2, NG)), dma((2, 2, NG)),
            dma((HEADS,)), dma((group,)),
            dma((ni,)), dma((ni,)),
            dma((npx,)), dma((HEADS,)),
            dma((npy,)), dma((npy,)),
        ],
        compiler_params=pltpu.CompilerParams(
            collective_id=0, has_side_effects=True, vmem_limit_bytes=48 * 2 ** 20
        ),
    )(queries[0], keys[0], values[0], pattern, targets, router_q, router_k)
    return attended[None], grad_q, grad_k


def solution(mesh):
    sizes = tuple(mesh.shape[a] for a in ("img", "py", "px"))
    return jax.shard_map(
        functools.partial(per_device, sizes),
        mesh=mesh,
        in_specs=(
            P("img", "py", "px", None),
            P("img", "py", "px", None),
            P("img", "py", "px", None),
            P("img", "py", "px", None),
            P("img", "py", "px", None, None),
            P(),
            P(),
        ),
        out_specs=(P("img", "py", "px", None), P(), P()),
        check_vma=False,
    )
```

time: 231 us -> 48.1 us (0.21)
  the two profiles are of different devices: /device:TPU:0 before, /device:TPU:17 now
where the time goes in v1:
time: 48.1 us; the launch traced here: 47.5 us
  Pallas kernels  35.5 us (74%)
  local copies, waits for them, and re-layouts  11.3 us (23%)
  between operations  0.7 us (1%)
    pallas_call x1, Pallas kernels, per_device(): pl.pallas_call(functools.partial(kernel, sizes), out_shape=(jax.ShapeDtyp...  35.5 us
    unnamed x24, local copies, waits for them, and re-layouts  11.3 us

profile of v1, /device:TPU:17, one launch (start us, length us, event | category | flops | bytes accessed | tf_op | source)
XLA Modules:
  0.0 47.5 jit_solution(11947210650035594295)
XLA Ops:
  0.6 0.0 copy-start.8
  0.6 0.8 %copy.10.tgt_ref = s32[1,2,2,12,3]{4,3,2,1,0:T(8,128)S(1)} copy(s32[1,2,2,12,3]{3,2,4,1,0:T(2,128)} %param.11) | data formatting | bytes 1152 | tf_op args[4]
  1.4 0.0 copy-start.1
  1.4 0.0 copy-start.2
  1.5 1.4 %copy.11.wq_ref = f32[12,128,64]{2,1,0:T(8,128)S(1)} copy(f32[12,128,64]{1,2,0:T(8,128)} %param.12) | data formatting | bytes 786432 | tf_op args[5]
  2.8 0.0 copy-start
  2.9 2.2 %copy.12.wk_ref = f32[12,128,64]{2,1,0:T(8,128)} copy(f32[12,128,64]{1,2,0:T(8,128)} %param.13) | data formatting | bytes 786432 | tf_op args[6]
  5.1 0.0 copy-done.8
  5.1 0.0 copy-done.1
  5.1 0.0 copy-done.2
  5.1 0.0 copy-done
  5.1 35.5 %shard_map.94 = (bf16[16,16,1536]{2,1,0:T(8,128)(2,1)S(1)}, f32[12,128,64]{2,1,0:T(8,128)S(1)}, f32[12,128,64]{2,1,0:T(8,128)S(1)}) custom-call(bf16[16,16,1536]{2,1,0:T(8,128)(2,1)S(1)} %bitcast.4, bf16[16,16,1536]{2,1,0:T(8,128)(2,1)S(1)} %bitcast.5, bf16[16,16,1536]{2,1,0:T(8,128)(2,1)S(1)} %bitcast.6, s32[1,2,2,9]{3,2,1,0:T(2,128)S(1)} %copy-done.8, ...), custom_call_target="tpu_custom_call" | custom-call | tf_op jit(solution)/shard_map/pallas_call | solution.py:544
  40.6 0.0 copy-start.3
  40.6 0.9 %copy-done.3 = bf16[16,16,1536]{2,1,0:T(8,128)(2,1)} copy-done((bf16[16,16,1536]{2,1,0:T(8,128)(2,1)}, bf16[16,16,1536]{2,1,0:T(8,128)(2,1)S(1)}, u32[]{:S(2)}) %copy-start.3) | copy-done | bytes 786456
  41.5 0.0 copy-start.5
  41.5 0.9 %copy-done.5 = f32[12,128,64]{2,1,0:T(8,128)} copy-done((f32[12,128,64]{2,1,0:T(8,128)}, f32[12,128,64]{2,1,0:T(8,128)S(1)}, u32[]{:S(2)}) %copy-start.5) | copy-done | bytes 393240
  42.3 0.0 copy-start.7
  42.3 0.9 %copy-done.7 = f32[12,128,64]{2,1,0:T(8,128)} copy-done((f32[12,128,64]{2,1,0:T(8,128)}, f32[12,128,64]{2,1,0:T(8,128)S(1)}, u32[]{:S(2)}) %copy-start.7) | copy-done | bytes 393240
  43.2 0.0 copy-start.6
  43.3 2.2 %copy.13 = f32[12,128,64]{1,2,0:T(8,128)} copy(f32[12,128,64]{2,1,0:T(8,128)} %copy-done.7) | data formatting | bytes 786432
  45.5 0.0 copy-done.6
  45.5 1.0 %copy.14 = f32[12,128,64]{1,2,0:T(8,128)} copy(f32[12,128,64]{2,1,0:T(8,128)S(1)} %copy-done.6) | data formatting | bytes 786432
  46.5 0.1 copy-done.4
  46.6 0.9 %copy.16 = bf16[1,16,16,1536]{3,2,1,0:T(8,128)(2,1)} copy(bf16[1,16,16,1536]{3,2,1,0:T(8,128)(2,1)S(1)} %bitcast.7) | data formatting | bytes 1572864
  (1 shorter events, 0.0 us)
Async XLA Ops:
  0.6 4.5 %copy-start.8 = (s32[1,2,2,9]{3,2,1,0:T(2,128)S(1)}, s32[1,2,2,9]{3,2,1,0:T(2,128)}, u32[]{:S(2)}) copy-start(s32[1,2,2,9]{3,2,1,0:T(2,128)} %pat_ref.1) | copy-start | bytes 436
  1.4 3.6 %copy-start.1 = (bf16[1,16,16,1536]{3,2,1,0:T(8,128)(2,1)S(1)}, bf16[1,16,16,1536]{3,2,1,0:T(8,128)(2,1)}, u32[]{:S(2)}) copy-start(bf16[1,16,16,1536]{3,2,1,0:T(8,128)(2,1)} %param.8) | copy-start | bytes 2359300
  1.4 3.6 %copy-start.2 = (bf16[1,16,16,1536]{3,2,1,0:T(8,128)(2,1)S(1)}, bf16[1,16,16,1536]{3,2,1,0:T(8,128)(2,1)}, u32[]{:S(2)}) copy-start(bf16[1,16,16,1536]{3,2,1,0:T(8,128)(2,1)} %param.9) | copy-start | bytes 2359300
  2.8 2.2 %copy-start = (bf16[1,16,16,1536]{3,2,1,0:T(8,128)(2,1)S(1)}, bf16[1,16,16,1536]{3,2,1,0:T(8,128)(2,1)}, u32[]{:S(2)}) copy-start(bf16[1,16,16,1536]{3,2,1,0:T(8,128)(2,1)} %param.7) | copy-start | bytes 2359300
  40.6 0.9 %copy-start.3 = (bf16[16,16,1536]{2,1,0:T(8,128)(2,1)}, bf16[16,16,1536]{2,1,0:T(8,128)(2,1)S(1)}, u32[]{:S(2)}) copy-start(bf16[16,16,1536]{2,1,0:T(8,128)(2,1)S(1)} %get-tuple-element.6) | copy-start | bytes 2359300
  41.5 0.9 %copy-start.5 = (f32[12,128,64]{2,1,0:T(8,128)}, f32[12,128,64]{2,1,0:T(8,128)S(1)}, u32[]{:S(2)}) copy-start(f32[12,128,64]{2,1,0:T(8,128)S(1)} %get-tuple-element.11) | copy-start | bytes 1179652
  42.3 0.9 %copy-start.7 = (f32[12,128,64]{2,1,0:T(8,128)}, f32[12,128,64]{2,1,0:T(8,128)S(1)}, u32[]{:S(2)}) copy-start(f32[12,128,64]{2,1,0:T(8,128)S(1)} %get-tuple-element.10) | copy-start | bytes 1179652
  43.2 2.2 %copy-start.6 = (f32[12,128,64]{2,1,0:T(8,128)S(1)}, f32[12,128,64]{2,1,0:T(8,128)}, u32[]{:S(2)}) copy-start(f32[12,128,64]{2,1,0:T(8,128)} %copy-done.5) | copy-start | bytes 1179652
  45.5 1.1 %copy-start.4 = (bf16[16,16,1536]{2,1,0:T(8,128)(2,1)S(1)}, bf16[16,16,1536]{2,1,0:T(8,128)(2,1)}, u32[]{:S(2)}) copy-start(bf16[16,16,1536]{2,1,0:T(8,128)(2,1)} %copy-done.3) | copy-start | bytes 2359300

commit v2 on v1

--- a/solution.py
+++ b/solution.py
@@ -17,7 +17,7 @@
 HG = 2
 NG = HEADS // HG
 GL = HG * DH
-WINDOW = 3
+WINDOW = 4
 BB = BS * BS
 DEAD = -1e30
 LIVE = 3e38
@@ -40,11 +40,12 @@
 
 
 def kernel(
-    sizes, q_ref, k_ref, v_ref, pat_ref, tgt_ref, wq_ref, wk_ref,
-    out_ref, gq_ref, gk_ref,
+    sizes, q_in, k_in, v_in, pat_ref, tgt_ref, wq_in, wk_in,
+    out_hbm, g_hbm,
+    q_ref, k_ref, v_ref, wq_s, wk_s, out_ref,
     q_s, zs, zr, yr, cr, acc, den, top, cap_a, cap_b, msg, pool, xbuf, gbuf,
     zs_sem, zr_sem, ys_sem, yr_sem, cs_sem, cr_sem,
-    ms_sem, mr_sem, xs_sem, xr_sem, gs_sem, gr_sem, hs_sem, hr_sem,
+    ms_sem, mr_sem, xs_sem, xr_sem, gs_sem, gr_sem, hs_sem, hr_sem, in_sem, out_sem,
 ):
     ni, npy, npx = sizes
     per_py = HEADS // npy
@@ -70,6 +71,22 @@
         pl.semaphore_signal(
             barrier, inc=1, device_id={"img": lax.rem(img + d, ni)}, device_id_type=MESH
         )
+
+    loads = [
+        pltpu.make_async_copy(a, b, in_sem.at[i])
+        for i, (a, b) in enumerate(((q_in, q_ref), (k_in, k_ref), (v_in, v_ref)))
+    ]
+    for load in loads:
+        load.start()
+    turn = lax.rem(px + npx * HEADS - py * per_py, npx)
+    own = turn < per_py
+    my_head = jnp.minimum(py * per_py + turn, HEADS - 1)
+    weights = [
+        pltpu.make_async_copy(wq_in.at[my_head], wq_s, in_sem.at[3]),
+        pltpu.make_async_copy(wk_in.at[my_head], wk_s, in_sem.at[4]),
+    ]
+    for load in weights:
+        load.start()
 
     def z_copy(side, g):
         return pltpu.make_async_remote_copy(
@@ -173,8 +190,6 @@
                 zs[side, g, 1, :, jl] = v[:, sl, :].reshape(2 * BB, DH).astype(BF16)
         return carry
 
-    lax.fori_loop(0, NG, prepare, 0)
-
     lane = lax.broadcasted_iota(jnp.int32, (1, DH), 1)
     code_rows = []
     for block in range(4):
@@ -188,9 +203,9 @@
     def encode(h, carry):
         for block in range(4):
             by, bx = divmod(block, 2)
-            chosen = lane == tgt_ref[0, by, bx, h, 0]
+            chosen = lane == tgt_ref[0, by, 0, bx, h]
             for t in range(1, TOPK):
-                chosen = chosen | (lane == tgt_ref[0, by, bx, h, t])
+                chosen = chosen | (lane == tgt_ref[0, by, t, bx, h])
             row = jnp.where(code_rows[block] < 0, F32(-1.0), jnp.where(chosen, F32(1.0), F32(0.0)))
             msg[h, 8 + block:9 + block, :] = row
         msg[h, 12:16, :] = jnp.zeros((4, DH), F32)
@@ -198,6 +213,10 @@
 
     lax.fori_loop(0, HEADS, encode, 0)
 
+    for load in loads:
+        load.wait()
+    lax.fori_loop(0, NG, prepare, 0)
+
     for side in range(2):
         @pl.when(jnp.logical_not(has_x[side]))
         def _():
@@ -229,9 +248,6 @@
         @pl.when(jnp.logical_not((py == oy) & (px == ox)))
         def _():
             m_copy(h, me).start()
-    turn = lax.rem(px + npx * HEADS - py * per_py, npx)
-    own = turn < per_py
-    my_head = jnp.minimum(py * per_py + turn, HEADS - 1)
 
     send_y(0)
     for g in range(1, WINDOW):
@@ -274,6 +290,9 @@
             device_id={"img": lax.rem(img + d, ni)}, device_id_type=MESH,
         )
 
+    for load in weights:
+        load.wait()
+
     @pl.when(own)
     def _():
         pool[me] = msg[my_head]
@@ -282,14 +301,14 @@
             def _():
                 m_copy(0, src).wait_recv()
         nb = 4 * group
-        pq = pool[:, 0:4, :].reshape(nb, DH) if False else jnp.concatenate(
-            [pool[s, 0:4, :] for s in range(group)], axis=0)
+        pq = jnp.concatenate([pool[s, 0:4, :] for s in range(group)], axis=0)
         pk = jnp.concatenate([pool[s, 4:8, :] for s in range(group)], axis=0)
         code = jnp.concatenate([pool[s, 8:12, :] for s in range(group)], axis=0)
-        wq = wq_ref[my_head]
-        wk = wk_ref[my_head]
-        rq = jnp.dot(pq, wq, precision=HIGH, preferred_element_type=F32)
-        rk = jnp.dot(pk, wk, precision=HIGH, preferred_element_type=F32)
+        rq, rk = [
+            lax.dot_general(
+                a, w[...], (((1,), (1,)), ((), ())), precision=HIGH, preferred_element_type=F32)
+            for a, w in ((pq, wq_s), (pk, wk_s))
+        ]
         logits = lax.dot_general(
             rq, rk, (((1,), (1,)), ((), ())), precision=HIGH, preferred_element_type=F32
         ) / math.sqrt(RW)
@@ -322,9 +341,9 @@
         grads = [
             lax.dot_general(
                 a, b, (((0,), (0,)), ((), ())), precision=HIGH, preferred_element_type=F32)
-            for a, b in ((pq, drq), (pk, drk))
+            for a, b in ((drq, pq), (drk, pk))
         ]
-        xbuf[img] = jnp.concatenate(grads, axis=1)
+        xbuf[img] = jnp.concatenate(grads, axis=0)
         for d in range(1, ni):
             x_copy(d).start()
 
@@ -391,10 +410,7 @@
                 g_copy(1, head).wait_recv()
 
     def finish_grads():
-        for h in range(HEADS):
-            g = gbuf[h].astype(F32)
-            gq_ref[h] = g[:, :RW]
-            gk_ref[h] = g[:, RW:]
+        pltpu.make_async_copy(gbuf, g_hbm, out_sem.at[NG]).start()
 
     def rim_heads(g):
         for j in range(HG):
@@ -450,6 +466,12 @@
             for by in range(2):
                 out_ref[by * BS:(by + 1) * BS, :, lanes(h * DH, DH)] = jnp.concatenate(
                     [outs[2 * by], outs[2 * by + 1]], axis=1).astype(BF16)
+        out_copy(g).start()
+
+    def out_copy(g):
+        gl = lanes(g * GL, GL)
+        return pltpu.make_async_copy(
+            out_ref.at[:, :, gl], out_hbm.at[:, :, gl], out_sem.at[g])
 
     def advance(s, carry):
         @pl.when(s < NG)
@@ -482,19 +504,19 @@
                         c_copy(side, side_x, g, side).wait_recv()
             rim_heads(g)
 
-        @pl.when(s == 0)
+        @pl.when(s == 1)
         def _():
             sum_images()
-        @pl.when(s == 2)
+        @pl.when(s == 3)
         def _():
             gather_px()
             cube_send(0)
         for step in range(1, len(bits)):
-            @pl.when(s == 2 + step)
+            @pl.when(s == 3 + step)
             def _():
                 cube_wait(step - 1)
                 cube_send(step)
-        @pl.when(s == 2 + len(bits))
+        @pl.when(s == 3 + len(bits))
         def _():
             cube_wait(len(bits) - 1)
             finish_grads()
@@ -515,9 +537,11 @@
                 @pl.when(has_y[side] & has_x[side_x])
                 def _():
                     c_copy(side, side_x, g, 1 - side).wait_send()
+        out_copy(g).wait()
         return carry
 
     lax.fori_loop(0, NG, drain, 0)
+    pltpu.make_async_copy(gbuf, g_hbm, out_sem.at[NG]).wait()
     for h in range(HEADS):
         oy, ox = owner_of(h)
         @pl.when(jnp.logical_not((py == oy) & (px == ox)))
@@ -539,18 +563,23 @@
     _, ty, tx, feat = queries.shape
     group = npy * npx
     dma = pltpu.SemaphoreType.DMA
-    vmem = pl.BlockSpec(memory_space=pltpu.VMEM)
+    away = pl.BlockSpec(memory_space=pl.ANY)
     smem = pl.BlockSpec(memory_space=pltpu.SMEM)
-    attended, grad_q, grad_k = pl.pallas_call(
+    attended, grads = pl.pallas_call(
         functools.partial(kernel, sizes),
         out_shape=(
             jax.ShapeDtypeStruct((ty, tx, feat), BF16),
-            jax.ShapeDtypeStruct((HEADS, DH, RW), F32),
-            jax.ShapeDtypeStruct((HEADS, DH, RW), F32),
+            jax.ShapeDtypeStruct((HEADS, 2 * RW, DH), BF16),
         ),
-        in_specs=[vmem, vmem, vmem, smem, smem, vmem, vmem],
-        out_specs=(vmem, vmem, vmem),
+        in_specs=[away, away, away, smem, smem, away, away],
+        out_specs=(away, away),
         scratch_shapes=[
+            pltpu.VMEM((ty, tx, feat), BF16),
+            pltpu.VMEM((ty, tx, feat), BF16),
+            pltpu.VMEM((ty, tx, feat), BF16),
+            pltpu.VMEM((RW, DH), F32),
+            pltpu.VMEM((RW, DH), F32),
+            pltpu.VMEM((ty, tx, feat), BF16),
             pltpu.VMEM((HEADS, 4 * BB, DH), BF16),
             pltpu.VMEM((2, NG, 2, 2 * BB, GL), BF16),
             pltpu.VMEM((2, NG, 2, 2 * BB, GL), BF16),
@@ -563,20 +592,25 @@
             pltpu.VMEM((4, BS, 6 * BB), F32),
             pltpu.VMEM((HEADS, 16, DH), F32),
             pltpu.VMEM((group, 16, DH), F32),
-            pltpu.VMEM((ni, DH, 2 * RW), F32),
-            pltpu.VMEM((HEADS, DH, 2 * RW), BF16),
+            pltpu.VMEM((ni, 2 * RW, DH), F32),
+            pltpu.VMEM((HEADS, 2 * RW, DH), BF16),
             dma((2, NG)), dma((2, NG)),
             dma((2, 2, NG)), dma((2, 2, NG)),
             dma((2, 2, NG)), dma((2, 2, NG)),
             dma((HEADS,)), dma((group,)),
             dma((ni,)), dma((ni,)),
             dma((npx,)), dma((HEADS,)),
-            dma((npy,)), dma((npy,)),
+            dma((npy,)), dma((npy,)), dma((5,)), dma((NG + 1,)),
         ],
         compiler_params=pltpu.CompilerParams(
-            collective_id=0, has_side_effects=True, vmem_limit_bytes=48 * 2 ** 20
+            collective_id=0, has_side_effects=True, vmem_limit_bytes=56 * 2 ** 20
         ),
-    )(queries[0], keys[0], values[0], pattern, targets, router_q, router_k)
+    )(
+        queries[0], keys[0], values[0], pattern, jnp.transpose(targets, (0, 1, 4, 2, 3)),
+        jnp.swapaxes(router_q, 1, 2), jnp.swapaxes(router_k, 1, 2),
+    )
+    grad_q, grad_k = [
+        jnp.swapaxes(grads[:, i * RW:(i + 1) * RW].astype(F32), 1, 2) for i in range(2)]
     return attended[None], grad_q, grad_k
 
 

time: 48.1 us -> 42.8 us (0.89)
  local copies, waits for them, and re-layouts: 11.3 us -> 0.88 us
  Pallas kernels: 35.5 us -> 39 us
  other arithmetic: 0 us -> 2.06 us
    unnamed x24 -> x3, local copies, waits for them, and re-layouts: 11.3 us -> 0.88 us
    pallas_call x1, Pallas kernels: 35.5 us -> 39 us  [per_device(): pl.pallas_call(functools.partial(kernel, sizes), out_shape=(jax.ShapeDtyp...]
    transpose x0 -> x1, other arithmetic: none -> 2.06 us  [per_device(): jnp.swapaxes(grads[:, i * RW:(i + 1) * RW].astype(F32), 1, 2)]
where the time goes in v2:
time: 42.8 us; the launch traced here: 42.6 us
  Pallas kernels  39 us (91%)
  other arithmetic  2.06 us (5%)
  local copies, waits for them, and re-layouts  0.88 us (2%)
  between operations  0.65 us (2%)
    pallas_call x1, Pallas kernels, per_device(): pl.pallas_call(functools.partial(kernel, sizes), out_shape=(jax.ShapeDtyp...  39 us
    transpose x1, other arithmetic, per_device(): jnp.swapaxes(grads[:, i * RW:(i + 1) * RW].astype(F32), 1, 2)  2.06 us
    unnamed x3, local copies, waits for them, and re-layouts  0.88 us

profile of v2, /device:TPU:17, one launch (start us, length us, event | category | flops | bytes accessed | tf_op | source)
XLA Modules:
  0.0 42.6 jit_solution(10860719434796602258)
XLA Ops:
  0.6 39.0 %shard_map.94 = (bf16[16,16,1536]{2,1,0:T(8,128)(2,1)}, bf16[12,128,128]{2,1,0:T(8,128)(2,1)}) custom-call(bf16[16,16,1536]{2,1,0:T(8,128)(2,1)} %bitcast.12, bf16[16,16,1536]{2,1,0:T(8,128)(2,1)} %bitcast.13, bf16[16,16,1536]{2,1,0:T(8,128)(2,1)} %bitcast.14, s32[1,2,2,9]{3,2,1,0:T(2,128)} %pat_ref.1, s32[1,2,3,2,12]{4,3,2,1,0:T(2,128)} %bitcast.17, ...), custom_call_target="tpu_custom_call" | custom-call | tf_op jit(solution)/shard_map/pallas_call | solution.py:568
  39.7 0.0 copy-start
  39.7 2.1 %convert_bitcast_fusion = (f32[12,128,64]{1,2,0:T(8,128)}, f32[12,128,64]{1,2,0:T(8,128)}) fusion(bf16[12,128,128]{2,1,0:T(8,128)(2,1)} %get-tuple-element.6), kind=kLoop, calls=%fused_computation | loop fusion | flops 196608 | bytes 1179648 | tf_op jit(solution)/shard_map/transpose | solution.py:613
  41.7 0.0 copy-done
  41.7 0.9 %copy.11 = bf16[1,16,16,1536]{3,2,1,0:T(8,128)(2,1)} copy(bf16[1,16,16,1536]{3,2,1,0:T(8,128)(2,1)S(1)} %bitcast.11) | data formatting | bytes 1572864
Async XLA Ops:
  39.7 2.1 %copy-start = (bf16[16,16,1536]{2,1,0:T(8,128)(2,1)S(1)}, bf16[16,16,1536]{2,1,0:T(8,128)(2,1)}, u32[]{:S(2)}) copy-start(bf16[16,16,1536]{2,1,0:T(8,128)(2,1)} %get-tuple-element.5) | copy-start | bytes 2359300

commit v3 on v2

--- a/solution.py
+++ b/solution.py
@@ -41,8 +41,8 @@
 
 def kernel(
     sizes, q_in, k_in, v_in, pat_ref, tgt_ref, wq_in, wk_in,
-    out_hbm, g_hbm,
-    q_ref, k_ref, v_ref, wq_s, wk_s, out_ref,
+    out_hbm, gq_hbm, gk_hbm,
+    q_ref, k_ref, v_ref, wq_s, wk_s, out_ref, gq_s, gk_s,
     q_s, zs, zr, yr, cr, acc, den, top, cap_a, cap_b, msg, pool, xbuf, gbuf,
     zs_sem, zr_sem, ys_sem, yr_sem, cs_sem, cr_sem,
     ms_sem, mr_sem, xs_sem, xr_sem, gs_sem, gr_sem, hs_sem, hr_sem, in_sem, out_sem,
@@ -74,7 +74,7 @@
 
     loads = [
         pltpu.make_async_copy(a, b, in_sem.at[i])
-        for i, (a, b) in enumerate(((q_in, q_ref), (k_in, k_ref), (v_in, v_ref)))
+        for i, (a, b) in enumerate(((k_in, k_ref), (v_in, v_ref), (q_in, q_ref)))
     ]
     for load in loads:
         load.start()
@@ -167,29 +167,6 @@
         else:
             cap_b[block, :, 256:384] = jnp.where(lane_b >= BB, corner, F32(DEAD))
 
-    def prepare(g, carry):
-        for j in range(HG):
-            h = g * HG + j
-            hl = lanes(h * DH, DH)
-            jl = pl.ds(j * DH, DH)
-            q = q_ref[:, :, hl].astype(F32)
-            k = k_ref[:, :, hl].astype(F32)
-            v = v_ref[:, :, hl].astype(F32)
-            parts = tile_blocks(q)
-            q_s[h] = jnp.concatenate([b.reshape(BB, DH) for b in parts], axis=0).astype(BF16)
-            for b in range(4):
-                msg[h, b:b + 1, :] = jnp.sum(
-                    jnp.sum(parts[b], axis=0), axis=0, keepdims=True) / BB
-            parts = tile_blocks(k)
-            for b in range(4):
-                msg[h, 4 + b:5 + b, :] = jnp.sum(
-                    jnp.sum(parts[b], axis=0), axis=0, keepdims=True) / BB
-            for side in range(2):
-                sl = slice(side * BS, (side + 1) * BS)
-                zs[side, g, 0, :, jl] = k[:, sl, :].reshape(2 * BB, DH).astype(BF16)
-                zs[side, g, 1, :, jl] = v[:, sl, :].reshape(2 * BB, DH).astype(BF16)
-        return carry
-
     lane = lax.broadcasted_iota(jnp.int32, (1, DH), 1)
     code_rows = []
     for block in range(4):
@@ -213,9 +190,63 @@
 
     lax.fori_loop(0, HEADS, encode, 0)
 
-    for load in loads:
-        load.wait()
+    def pack(g):
+        for which, ref in enumerate((k_ref, v_ref)):
+            x = ref[:, :, lanes(g * GL, GL)].astype(F32)
+            for side in range(2):
+                zs[side, g, which] = x[:, side * BS:(side + 1) * BS, :].reshape(
+                    2 * BB, GL).astype(BF16)
+
+    def prepare(g, carry):
+        for j in range(HG):
+            h = g * HG + j
+            hl = lanes(h * DH, DH)
+            for at, ref in enumerate((q_ref, k_ref)):
+                parts = tile_blocks(ref[:, :, hl].astype(F32))
+                if at == 0:
+                    q_s[h] = jnp.concatenate(
+                        [b.reshape(BB, DH) for b in parts], axis=0).astype(BF16)
+                for b in range(4):
+                    msg[h, 4 * at + b:4 * at + b + 1, :] = jnp.sum(
+                        jnp.sum(parts[b], axis=0), axis=0, keepdims=True) / BB
+        return carry
+
+    loads[0].wait()
+    loads[1].wait()
+    pack(0)
+    pl.semaphore_wait(barrier, group - 1 + ni - 1)
+    send_z(0)
+    send_y(0)
+    loads[2].wait()
     lax.fori_loop(0, NG, prepare, 0)
+
+    def owner_of(h):
+        return h // per_py, h % npx
+
+    def m_copy(h, slot):
+        oy, ox = owner_of(h)
+        return pltpu.make_async_remote_copy(
+            src_ref=msg.at[h], dst_ref=pool.at[slot],
+            send_sem=ms_sem.at[h], recv_sem=mr_sem.at[slot],
+            device_id={"py": oy, "px": ox}, device_id_type=MESH,
+        )
+
+    for h in range(HEADS):
+        oy, ox = owner_of(h)
+        @pl.when(jnp.logical_not((py == oy) & (px == ox)))
+        def _():
+            m_copy(h, me).start()
+
+    def pack_and_send(g, carry):
+        pack(g)
+
+        @pl.when(g < WINDOW)
+        def _():
+            send_z(g)
+            send_y(g)
+        return carry
+
+    lax.fori_loop(1, NG, pack_and_send, 0)
 
     for side in range(2):
         @pl.when(jnp.logical_not(has_x[side]))
@@ -229,30 +260,6 @@
             def _():
                 cr[side, other] = jnp.zeros(cr.shape[2:], BF16)
 
-    pl.semaphore_wait(barrier, group - 1 + ni - 1)
-    send_z(0)
-
-    def owner_of(h):
-        return h // per_py, h % npx
-
-    def m_copy(h, slot):
-        oy, ox = owner_of(h)
-        return pltpu.make_async_remote_copy(
-            src_ref=msg.at[h], dst_ref=pool.at[slot],
-            send_sem=ms_sem.at[h], recv_sem=mr_sem.at[slot],
-            device_id={"py": oy, "px": ox}, device_id_type=MESH,
-        )
-
-    for h in range(HEADS):
-        oy, ox = owner_of(h)
-        @pl.when(jnp.logical_not((py == oy) & (px == ox)))
-        def _():
-            m_copy(h, me).start()
-
-    send_y(0)
-    for g in range(1, WINDOW):
-        send_z(g)
-        send_y(g)
 
     scale = math.log2(math.e) / math.sqrt(DH)
     ones = jnp.ones((2 * DH, DH), BF16)
@@ -273,7 +280,25 @@
             top[h] = jnp.broadcast_to(m, (4 * BB, DH))
         return carry
 
+    def forward(s):
+        for side in range(2):
+            @pl.when(has_x[side])
+            def _():
+                z_arrival(side, s).wait_recv()
+            for side_y in range(2):
+                @pl.when(has_x[side] & has_y[side_y])
+                def _():
+                    c_copy(side_y, side, s, 1 - side_y).start()
+
+        @pl.when(s + WINDOW < NG)
+        def _():
+            send_z(s + WINDOW)
+            send_y(s + WINDOW)
+
     lax.fori_loop(0, NG // 2, local_heads, 0)
+    forward(0)
+    lax.fori_loop(NG // 2, NG, local_heads, 0)
+    forward(1)
 
     def x_copy(d):
         return pltpu.make_async_remote_copy(
@@ -347,8 +372,6 @@
         for d in range(1, ni):
             x_copy(d).start()
 
-    lax.fori_loop(NG // 2, NG, local_heads, 0)
-
     def g_copy(d, head):
         return pltpu.make_async_remote_copy(
             src_ref=gbuf.at[head], dst_ref=gbuf.at[head],
@@ -410,7 +433,20 @@
                 g_copy(1, head).wait_recv()
 
     def finish_grads():
-        pltpu.make_async_copy(gbuf, g_hbm, out_sem.at[NG]).start()
+        def widen(h, carry):
+            gq_s[h] = gbuf[h, 0:RW, :].astype(F32)
+            gk_s[h] = gbuf[h, RW:2 * RW, :].astype(F32)
+            return carry
+
+        lax.fori_loop(0, HEADS, widen, 0)
+        for store in grad_copies():
+            store.start()
+
+    def grad_copies():
+        return [
+            pltpu.make_async_copy(gq_s, gq_hbm, out_sem.at[NG]),
+            pltpu.make_async_copy(gk_s, gk_hbm, out_sem.at[NG + 1]),
+        ]
 
     def rim_heads(g):
         for j in range(HG):
@@ -474,35 +510,21 @@
             out_ref.at[:, :, gl], out_hbm.at[:, :, gl], out_sem.at[g])
 
     def advance(s, carry):
-        @pl.when(s < NG)
-        def _():
-            for side in range(2):
-                @pl.when(has_x[side])
+        @pl.when((s >= 2) & (s < NG))
+        def _():
+            forward(s)
+
+        g = s - 1
+        for side in range(2):
+            @pl.when(has_y[side])
+            def _():
+                for which in range(2):
+                    y_copy(which, side, g, side).wait_recv()
+            for side_x in range(2):
+                @pl.when(has_y[side] & has_x[side_x])
                 def _():
-                    z_arrival(side, s).wait_recv()
-                for side_y in range(2):
-                    @pl.when(has_x[side] & has_y[side_y])
-                    def _():
-                        c_copy(side_y, side, s, 1 - side_y).start()
-
-            @pl.when(s + WINDOW < NG)
-            def _():
-                send_z(s + WINDOW)
-                send_y(s + WINDOW)
-
-        @pl.when(s >= 1)
-        def _():
-            g = s - 1
-            for side in range(2):
-                @pl.when(has_y[side])
-                def _():
-                    for which in range(2):
-                        y_copy(which, side, g, side).wait_recv()
-                for side_x in range(2):
-                    @pl.when(has_y[side] & has_x[side_x])
-                    def _():
-                        c_copy(side, side_x, g, side).wait_recv()
-            rim_heads(g)
+                    c_copy(side, side_x, g, side).wait_recv()
+        rim_heads(g)
 
         @pl.when(s == 1)
         def _():
@@ -522,7 +544,7 @@
             finish_grads()
         return carry
 
-    lax.fori_loop(0, NG + 1, advance, 0)
+    lax.fori_loop(1, NG + 1, advance, 0)
 
     def drain(g, carry):
         for side in range(2):
@@ -541,7 +563,8 @@
         return carry
 
     lax.fori_loop(0, NG, drain, 0)
-    pltpu.make_async_copy(gbuf, g_hbm, out_sem.at[NG]).wait()
+    for store in grad_copies():
+        store.wait()
     for h in range(HEADS):
         oy, ox = owner_of(h)
         @pl.when(jnp.logical_not((py == oy) & (px == ox)))
@@ -565,14 +588,15 @@
     dma = pltpu.SemaphoreType.DMA
     away = pl.BlockSpec(memory_space=pl.ANY)
     smem = pl.BlockSpec(memory_space=pltpu.SMEM)
-    attended, grads = pl.pallas_call(
+    attended, grad_q, grad_k = pl.pallas_call(
         functools.partial(kernel, sizes),
         out_shape=(
             jax.ShapeDtypeStruct((ty, tx, feat), BF16),
-            jax.ShapeDtypeStruct((HEADS, 2 * RW, DH), BF16),
+            jax.ShapeDtypeStruct((HEADS, RW, DH), F32),
+            jax.ShapeDtypeStruct((HEADS, RW, DH), F32),
         ),
         in_specs=[away, away, away, smem, smem, away, away],
-        out_specs=(away, away),
+        out_specs=(away, away, away),
         scratch_shapes=[
             pltpu.VMEM((ty, tx, feat), BF16),
             pltpu.VMEM((ty, tx, feat), BF16),
@@ -580,6 +604,8 @@
             pltpu.VMEM((RW, DH), F32),
             pltpu.VMEM((RW, DH), F32),
             pltpu.VMEM((ty, tx, feat), BF16),
+            pltpu.VMEM((HEADS, RW, DH), F32),
+            pltpu.VMEM((HEADS, RW, DH), F32),
             pltpu.VMEM((HEADS, 4 * BB, DH), BF16),
             pltpu.VMEM((2, NG, 2, 2 * BB, GL), BF16),
             pltpu.VMEM((2, NG, 2, 2 * BB, GL), BF16),
@@ -600,7 +626,7 @@
             dma((HEADS,)), dma((group,)),
             dma((ni,)), dma((ni,)),
             dma((npx,)), dma((HEADS,)),
-            dma((npy,)), dma((npy,)), dma((5,)), dma((NG + 1,)),
+            dma((npy,)), dma((npy,)), dma((5,)), dma((NG + 2,)),
         ],
         compiler_params=pltpu.CompilerParams(
             collective_id=0, has_side_effects=True, vmem_limit_bytes=56 * 2 ** 20
@@ -609,9 +635,7 @@
         queries[0], keys[0], values[0], pattern, jnp.transpose(targets, (0, 1, 4, 2, 3)),
         jnp.swapaxes(router_q, 1, 2), jnp.swapaxes(router_k, 1, 2),
     )
-    grad_q, grad_k = [
-        jnp.swapaxes(grads[:, i * RW:(i + 1) * RW].astype(F32), 1, 2) for i in range(2)]
-    return attended[None], grad_q, grad_k
+    return attended[None], jnp.swapaxes(grad_q, 1, 2), jnp.swapaxes(grad_k, 1, 2)
 
 
 def solution(mesh):

time: 42.8 us -> 43.9 us (1.026)
  local copies, waits for them, and re-layouts: 0.88 us -> 4 us
  other arithmetic: 2.06 us -> 0 us
    unnamed x3 -> x7, local copies, waits for them, and re-layouts: 0.88 us -> 4 us
    transpose x1 -> x0, other arithmetic: 2.06 us -> none  [per_device(): jnp.swapaxes(grads[:, i * RW:(i + 1) * RW].astype(F32), 1, 2)]
where the time goes in v3:
time: 43.9 us; the launch traced here: 43.7 us
  Pallas kernels  39 us (89%)
  local copies, waits for them, and re-layouts  4 us (9%)
  between operations  0.65 us (1%)
    pallas_call x1, Pallas kernels, per_device(): pl.pallas_call(functools.partial(kernel, sizes), out_shape=(jax.ShapeDtyp...  39 us
    unnamed x7, local copies, waits for them, and re-layouts  4 us

profile of v3, /device:TPU:17, one launch (start us, length us, event | category | flops | bytes accessed | tf_op | source)
XLA Modules:
  0.0 43.7 jit_solution(11105313113834450073)
XLA Ops:
  0.6 39.0 %shard_map.94 = (bf16[16,16,1536]{2,1,0:T(8,128)(2,1)}, f32[12,64,128]{2,1,0:T(8,128)}, f32[12,64,128]{2,1,0:T(8,128)}) custom-call(bf16[16,16,1536]{2,1,0:T(8,128)(2,1)} %bitcast.10, bf16[16,16,1536]{2,1,0:T(8,128)(2,1)} %bitcast.11, bf16[16,16,1536]{2,1,0:T(8,128)(2,1)} %bitcast.12, s32[1,2,2,9]{3,2,1,0:T(2,128)} %pat_ref.1, s32[1,2,3,2,12]{4,3,2,1,0:T(2,128)} %bitcast.17, ...), custom_call_target="tpu_custom_call" | custom-call | tf_op jit(solution)/shard_map/pallas_call | solution.py:591
  39.7 0.0 copy-start.1
  39.7 2.1 %copy.13 = bf16[1,16,16,1536]{3,2,1,0:T(8,128)(2,1)} copy(bf16[1,16,16,1536]{3,2,1,0:T(8,128)(2,1)} %bitcast.9) | data formatting | bytes 1572864
  41.8 0.0 copy-done.1
  41.8 0.0 copy-start
  41.8 0.7 %copy.14 = f32[12,128,64]{1,2,0:T(8,128)} copy(f32[12,128,64]{1,2,0:T(8,128)S(1)} %bitcast.16) | data formatting | bytes 786432
  42.5 0.4 copy-done
  42.9 0.7 %copy.15 = f32[12,128,64]{1,2,0:T(8,128)} copy(f32[12,128,64]{1,2,0:T(8,128)S(1)} %bitcast.15) | data formatting | bytes 786432
Async XLA Ops:
  39.7 2.1 %copy-start.1 = (f32[12,64,128]{2,1,0:T(8,128)S(1)}, f32[12,64,128]{2,1,0:T(8,128)}, u32[]{:S(2)}) copy-start(f32[12,64,128]{2,1,0:T(8,128)} %get-tuple-element.7) | copy-start | bytes 1179652
  41.8 1.1 %copy-start = (f32[12,64,128]{2,1,0:T(8,128)S(1)}, f32[12,64,128]{2,1,0:T(8,128)}, u32[]{:S(2)}) copy-start(f32[12,64,128]{2,1,0:T(8,128)} %get-tuple-element.8) | copy-start | bytes 1179652

commit v4 on v3

--- a/solution.py
+++ b/solution.py
@@ -14,10 +14,10 @@
 BS = 8
 TOPK = 3
 NOFF = 9
-HG = 2
+HG = 3
 NG = HEADS // HG
 GL = HG * DH
-WINDOW = 4
+WINDOW = 3
 BB = BS * BS
 DEAD = -1e30
 LIVE = 3e38
@@ -295,9 +295,9 @@
             send_z(s + WINDOW)
             send_y(s + WINDOW)
 
-    lax.fori_loop(0, NG // 2, local_heads, 0)
+    lax.fori_loop(0, NG // 2, local_heads, 0, unroll=True)
     forward(0)
-    lax.fori_loop(NG // 2, NG, local_heads, 0)
+    lax.fori_loop(NG // 2, NG, local_heads, 0, unroll=True)
     forward(1)
 
     def x_copy(d):
@@ -529,16 +529,16 @@
         @pl.when(s == 1)
         def _():
             sum_images()
-        @pl.when(s == 3)
+        @pl.when(s == 2)
         def _():
             gather_px()
             cube_send(0)
         for step in range(1, len(bits)):
-            @pl.when(s == 3 + step)
+            @pl.when(s == 2 + step)
             def _():
                 cube_wait(step - 1)
                 cube_send(step)
-        @pl.when(s == 3 + len(bits))
+        @pl.when(s == 2 + len(bits))
         def _():
             cube_wait(len(bits) - 1)
             finish_grads()
@@ -579,6 +579,22 @@
     for step in range(len(bits)):
         for r, slot in zip(held(step), slots(step)):
             h_copy(bits[step], r * per_py, per_py, slot).wait_send()
+
+
+def hand_over(*refs):
+    half = (len(refs) - 1) // 2
+    sems = refs[-1]
+    copies, at = [], 0
+    for src, dst in zip(refs[:half], refs[half:-1]):
+        step = src.shape[0] // 4
+        for i in range(4):
+            rows = pl.ds(i * step, step)
+            copies.append(pltpu.make_async_copy(src.at[rows], dst.at[rows], sems.at[at]))
+            at += 1
+    for copy in copies:
+        copy.start()
+    for copy in copies:
+        copy.wait()
 
 
 def per_device(sizes, queries, keys, values, pattern, targets, router_q, router_k):
@@ -635,6 +651,15 @@
         queries[0], keys[0], values[0], pattern, jnp.transpose(targets, (0, 1, 4, 2, 3)),
         jnp.swapaxes(router_q, 1, 2), jnp.swapaxes(router_k, 1, 2),
     )
+    made = (attended, grad_q, grad_k)
+    attended, grad_q, grad_k = pl.pallas_call(
+        hand_over,
+        out_shape=tuple(jax.ShapeDtypeStruct(a.shape, a.dtype) for a in made),
+        in_specs=[away] * 3,
+        out_specs=(away,) * 3,
+        scratch_shapes=[dma((12,))],
+        compiler_params=pltpu.CompilerParams(vmem_limit_bytes=56 * 2 ** 20),
+    )(*made)
     return attended[None], jnp.swapaxes(grad_q, 1, 2), jnp.swapaxes(grad_k, 1, 2)
 
 

time: 43.9 us -> 86.7 us (1.97)
  the two profiles are of different devices: /device:TPU:17 before, /device:TPU:1 now
where the time goes in v4:
time: 86.7 us; the launch traced here: 86.5 us
  Pallas kernels  85.9 us (99%)
    pallas_call x1, Pallas kernels, per_device(): pl.pallas_call(hand_over, out_shape=tuple((jax.ShapeDtypeStruct(a.shape,...  48.9 us
    pallas_call x1, Pallas kernels, per_device(): pl.pallas_call(functools.partial(kernel, sizes), out_shape=(jax.ShapeDtyp...  37 us

profile of v4, /device:TPU:1, one launch (start us, length us, event | category | flops | bytes accessed | tf_op | source)
XLA Modules:
  0.0 86.5 jit_solution(5300525715518067181)
XLA Ops:
  0.6 37.0 %shard_map.94 = (bf16[16,16,1536]{2,1,0:T(8,128)(2,1)}, f32[12,64,128]{2,1,0:T(8,128)}, f32[12,64,128]{2,1,0:T(8,128)}) custom-call(bf16[16,16,1536]{2,1,0:T(8,128)(2,1)} %bitcast.9, bf16[16,16,1536]{2,1,0:T(8,128)(2,1)} %bitcast.10, bf16[16,16,1536]{2,1,0:T(8,128)(2,1)} %bitcast.11, s32[1,2,2,9]{3,2,1,0:T(2,128)} %pat_ref.1, s32[1,2,3,2,12]{4,3,2,1,0:T(2,128)} %bitcast.14, ...), custom_call_target="tpu_custom_call" | custom-call | tf_op jit(solution)/shard_map/pallas_call | solution.py:607
  37.7 48.9 %shard_map.95 = (bf16[16,16,1536]{2,1,0:T(8,128)(2,1)}, f32[12,64,128]{2,1,0:T(8,128)}, f32[12,64,128]{2,1,0:T(8,128)}) custom-call(bf16[16,16,1536]{2,1,0:T(8,128)(2,1)} %get-tuple-element.9.refs_0_, f32[12,64,128]{2,1,0:T(8,128)} %get-tuple-element.10.refs_1_, f32[12,64,128]{2,1,0:T(8,128)} %get-tuple-element.11.refs_2_), custom_call_target="tpu_custom_call" | custom-call | tf_op jit(solution)/shard_map/pallas_call | solution.py:655

commit v5 on v4

--- a/solution.py
+++ b/solution.py
@@ -582,19 +582,25 @@
 
 
 def hand_over(*refs):
-    half = (len(refs) - 1) // 2
-    sems = refs[-1]
-    copies, at = [], 0
-    for src, dst in zip(refs[:half], refs[half:-1]):
+    count = len(refs) // 3
+    come, go = refs[-2:]
+    pieces, at = [], 0
+    for src, dst, mid in zip(refs[:count], refs[count:2 * count], refs[2 * count:-2]):
         step = src.shape[0] // 4
         for i in range(4):
             rows = pl.ds(i * step, step)
-            copies.append(pltpu.make_async_copy(src.at[rows], dst.at[rows], sems.at[at]))
+            pieces.append((
+                pltpu.make_async_copy(src.at[rows], mid.at[rows], come.at[at]),
+                pltpu.make_async_copy(mid.at[rows], dst.at[rows], go.at[at]),
+            ))
             at += 1
-    for copy in copies:
-        copy.start()
-    for copy in copies:
-        copy.wait()
+    for first, _ in pieces:
+        first.start()
+    for first, second in pieces:
+        first.wait()
+        second.start()
+    for _, second in pieces:
+        second.wait()
 
 
 def per_device(sizes, queries, keys, values, pattern, targets, router_q, router_k):
@@ -657,7 +663,7 @@
         out_shape=tuple(jax.ShapeDtypeStruct(a.shape, a.dtype) for a in made),
         in_specs=[away] * 3,
         out_specs=(away,) * 3,
-        scratch_shapes=[dma((12,))],
+        scratch_shapes=[pltpu.VMEM(a.shape, a.dtype) for a in made] + [dma((12,)), dma((12,))],
         compiler_params=pltpu.CompilerParams(vmem_limit_bytes=56 * 2 ** 20),
     )(*made)
     return attended[None], jnp.swapaxes(grad_q, 1, 2), jnp.swapaxes(grad_k, 1, 2)

time: 86.7 us -> 40.3 us (0.46)
  Pallas kernels: 85.9 us -> 39.4 us
    pallas_call x1, Pallas kernels: 48.9 us -> 2.36 us  [per_device(): pl.pallas_call(hand_over, out_shape=tuple((jax.ShapeDtypeStruct(a.shape,...]
where the time goes in v5:
time: 40.3 us; the launch traced here: 40 us
  Pallas kernels  39.4 us (98%)
  between operations  0.64 us (2%)
    pallas_call x1, Pallas kernels, per_device(): pl.pallas_call(functools.partial(kernel, sizes), out_shape=(jax.ShapeDtyp...  37 us
    pallas_call x1, Pallas kernels, per_device(): pl.pallas_call(hand_over, out_shape=tuple((jax.ShapeDtypeStruct(a.shape,...  2.36 us

profile of v5, /device:TPU:1, one launch (start us, length us, event | category | flops | bytes accessed | tf_op | source)
XLA Modules:
  0.0 40.0 jit_solution(8688442076140324128)
XLA Ops:
  0.6 37.0 %shard_map.94 = (bf16[16,16,1536]{2,1,0:T(8,128)(2,1)}, f32[12,64,128]{2,1,0:T(8,128)}, f32[12,64,128]{2,1,0:T(8,128)}) custom-call(bf16[16,16,1536]{2,1,0:T(8,128)(2,1)} %bitcast.9, bf16[16,16,1536]{2,1,0:T(8,128)(2,1)} %bitcast.10, bf16[16,16,1536]{2,1,0:T(8,128)(2,1)} %bitcast.11, s32[1,2,2,9]{3,2,1,0:T(2,128)} %pat_ref.1, s32[1,2,3,2,12]{4,3,2,1,0:T(2,128)} %bitcast.14, ...), custom_call_target="tpu_custom_call" | custom-call | tf_op jit(solution)/shard_map/pallas_call | solution.py:613
  37.7 2.4 %shard_map.95 = (bf16[16,16,1536]{2,1,0:T(8,128)(2,1)}, f32[12,64,128]{2,1,0:T(8,128)}, f32[12,64,128]{2,1,0:T(8,128)}) custom-call(bf16[16,16,1536]{2,1,0:T(8,128)(2,1)} %get-tuple-element.9.refs_0_, f32[12,64,128]{2,1,0:T(8,128)} %get-tuple-element.10.refs_1_, f32[12,64,128]{2,1,0:T(8,128)} %get-tuple-element.11.refs_2_), custom_call_target="tpu_custom_call" | custom-call | tf_op jit(solution)/shard_map/pallas_call | solution.py:661
